TPU v7x, 256 devices: a whole 4x4x8 slice. The times are simulated.
256 devices in a mesh: dp: 16 (over z, core), seq: 8 (over x, y_lo), section: 2 (over y_hi).
Axes of the slice: x: 4, y: 4 (y_hi: 2, y_lo: 2; y = y_hi * 2 + y_lo), z: 8, core: 2. Of those that a mesh axis runs over, the one named last changes fastest.
Arguments:
- queries: bfloat16 [2, 16, 1024, 2048], P('section', 'dp', 'seq'), may hold values from -6 to 6
- key_values: bfloat16 [2, 16, 2, 1024, 2048], P('section', 'dp', None, 'seq'), may hold values from -18 to 18
- resid: bfloat16 [2, 16, 1024, 2048], P('section', 'dp', 'seq'), may hold values from -6 to 6
- upstream: bfloat16 [2, 16, 1024, 2048], P('section', 'dp', 'seq'), may hold values from -6 to 6
- w_out: bfloat16 [2, 2048, 2048], P('section', 'dp'), may hold values from -1 to 1
- gain: float32 [2, 2048], P('section'), may hold values from 0.25 to 1.75
- global_ids: int32 [16, 2], P('dp'), may hold values from 0 to 15, as said below
- random_ids: int32 [16, 16, 3], P('dp'), may hold values from 0 to 15, as said below
Outputs:
- grad_queries: bfloat16 [2, 16, 1024, 2048], P('section', 'dp', 'seq')
- grad_key_values: bfloat16 [2, 16, 2, 1024, 2048], P('section', 'dp', None, 'seq')
- passed: bfloat16 [2, 16, 1024, 2048], P('section', 'dp', 'seq')
- grad_w_out: float32 [2, 2048, 2048], P('section', 'dp')
Inputs may be any that keep to these rules, and one draw needn't show every extreme that they name: `global_ids`: the 2 blocks of one sequence are different. `random_ids`: for each sequence, the 6 entries of the query blocks of one segment name blocks of any one segment at most 1 times.
All inputs are finite; a program needn't handle non-finite values.
Results may differ from a plain program's by a relative error of at most 0.025.
Values may be sent and summed in bfloat16 or wider, within the bound.
No kernel may reach another device: no remote copies, remote signals or barrier semaphores. Data moves between devices by JAX's collectives and lax.ppermute only.
A program may use at most 128 MiB of HBM per device.

v0:
```python
import math

import jax
import jax.numpy as jnp
from jax import lax
from jax.sharding import PartitionSpec as P

HDIM = 128
BLOCK = 64
R = 3
NG = 2


def from_root(block, axis, holder):
    block = jnp.where(lax.axis_index(axis) == holder, block, jnp.zeros_like(block))
    return lax.psum(block, axis)


def padded(cells, sides, width):
    for axis, dim in sides:
        count = lax.axis_size(axis)
        ends = count - 1
        head = lax.slice_in_dim(cells, 0, width, axis=dim)
        tail = lax.slice_in_dim(cells, cells.shape[dim] - width, cells.shape[dim], axis=dim)
        cells = jnp.concatenate(
            [
                lax.ppermute(tail, axis, [(i, (i + 1) % count) for i in range(ends)]),
                cells,
                lax.ppermute(head, axis, [((i + 1) % count, i) for i in range(ends)]),
            ],
            axis=dim,
        )
    return cells


def passed_along(block, axis, distance):
    devices = range(lax.axis_size(axis))
    route = [((i - distance) % len(devices), i) for i in devices]
    return lax.ppermute(block, axis, route)


def softmax_rows(scores, valid):
    masked = jnp.where(valid, scores, -1e30)
    top = jnp.max(masked, axis=-1, keepdims=True)
    raised = jnp.exp(masked - top)
    total = jnp.sum(raised, axis=-1, keepdims=True)
    return raised / total


def on_device(queries, key_values, resid, upstream, w_out, gain, global_ids, random_ids):
    own_query = queries[0, 0]
    pairs = key_values[0, 0]
    inputs = resid[0, 0]
    grad_out = upstream[0, 0]
    w_shard = w_out[0]
    gain_row = gain[0]
    glob_ids = global_ids[0]
    rand_ids = random_ids[0]
    tokens, width = own_query.shape
    seq_count = lax.axis_size("seq")
    seq_index = lax.axis_index("seq")
    blocks = tokens // BLOCK
    heads = width // HDIM
    slots = blocks * R
    capacity = (slots + seq_count - 1) // seq_count
    listed = 3 + NG + R
    scale = 1.0 / math.sqrt(HDIM)
    own_blocks = pairs.reshape(2, blocks, BLOCK, width)
    glob_owner = glob_ids // blocks
    glob_local = glob_ids % blocks
    pick_table = glob_local[:, None] == jnp.arange(blocks)[None, :]
    owned = pick_table & (glob_owner == seq_index)[:, None]
    picked_rows = []
    for which in range(NG):
        chosen = jnp.einsum(
            "q,cqax->cax",
            pick_table[which].astype(jnp.bfloat16),
            own_blocks,
            preferred_element_type=jnp.float32,
        ).astype(jnp.bfloat16)
        picked_rows.append(from_root(chosen, "seq", glob_owner[which]))
    glob_blocks = jnp.stack(picked_rows, axis=1)
    dest_ids = rand_ids.reshape(seq_count, slots)
    dest_owner = dest_ids // blocks
    dest_local = dest_ids % blocks
    mine = dest_owner == seq_index
    dest_rank = jnp.cumsum(mine.astype(jnp.int32), axis=1) - 1
    position = jnp.arange(capacity)
    routed = (mine[:, None, :] & (dest_rank[:, None, :] == position[None, :, None])).astype(
        jnp.int32
    )
    local_hot = (dest_local[:, :, None] == jnp.arange(blocks)[None, None, :]).astype(jnp.int32)
    send_table = (
        jnp.einsum("dcs,dsq->dcq", routed, local_hot)
        .reshape(seq_count * capacity, blocks)
        .astype(jnp.bfloat16)
    )
    outgoing = jnp.einsum(
        "mq,cqax->cmax", send_table, own_blocks, preferred_element_type=jnp.float32
    ).astype(jnp.bfloat16)
    incoming = lax.all_to_all(outgoing, "seq", split_axis=1, concat_axis=1, tiled=True)
    my_ids = lax.dynamic_slice_in_dim(rand_ids, seq_index * blocks, blocks, 0).reshape(slots)
    my_owner = my_ids // blocks
    same = my_owner[:, None] == my_owner[None, :]
    earlier = jnp.arange(slots)[None, :] < jnp.arange(slots)[:, None]
    my_rank = jnp.sum((same & earlier).astype(jnp.int32), axis=1)
    recv_table = (
        (my_owner * capacity + my_rank)[:, None] == jnp.arange(seq_count * capacity)[None, :]
    ).astype(jnp.bfloat16)
    rand_blocks = jnp.einsum(
        "sm,cmax->csax", recv_table, incoming, preferred_element_type=jnp.float32
    ).astype(jnp.bfloat16)
    extended = padded(pairs, (("seq", 1),), BLOCK)
    ext_blocks = extended.reshape(2, blocks + 2, BLOCK, width)
    window_list = jnp.stack(
        [ext_blocks[:, 0:blocks], ext_blocks[:, 1 : blocks + 1], ext_blocks[:, 2 : blocks + 2]],
        axis=2,
    )
    glob_list = jnp.broadcast_to(glob_blocks[:, None], (2, blocks, NG, BLOCK, width))
    rand_list = rand_blocks.reshape(2, blocks, R, BLOCK, width)
    gathered = jnp.concatenate([window_list, glob_list, rand_list], axis=2)
    key_list = gathered[0].reshape(blocks, listed * BLOCK, heads, HDIM)
    value_list = gathered[1].reshape(blocks, listed * BLOCK, heads, HDIM)
    window_idx = jnp.arange(blocks)[:, None] + jnp.arange(3)[None, :]
    window_block = seq_index * blocks + window_idx - 1
    window_valid = (window_block >= 0) & (window_block < seq_count * blocks)
    valid_blocks = jnp.concatenate([window_valid, jnp.ones((blocks, NG + R), bool)], axis=1)
    valid = jnp.repeat(valid_blocks, BLOCK, axis=1)[:, None, None, :]
    query_blocks = own_query.reshape(blocks, BLOCK, heads, HDIM)
    scores = (
        jnp.einsum("jahe,jthe->jhat", query_blocks, key_list, preferred_element_type=jnp.float32)
        * scale
    )
    shares = softmax_rows(scores, valid)
    shares_low = shares.astype(jnp.bfloat16)
    attended = jnp.einsum(
        "jhat,jthe->jahe", shares_low, value_list, preferred_element_type=jnp.float32
    )
    attended = attended.astype(jnp.bfloat16).reshape(tokens, width)
    w_full = lax.all_gather(w_shard, "dp", axis=0, tiled=True)
    projected = jnp.dot(attended, w_full, preferred_element_type=jnp.float32)
    summed = inputs.astype(jnp.float32) + projected
    inverse = lax.rsqrt(jnp.mean(summed * summed, axis=-1, keepdims=True) + 1e-06)
    scaled_grad = grad_out.astype(jnp.float32) * gain_row
    inner = jnp.mean(scaled_grad * summed, axis=-1, keepdims=True)
    grad_sum = (inverse * scaled_grad - summed * inverse**3 * inner).astype(jnp.bfloat16)
    passed = passed_along(grad_sum, "section", -1)
    grad_attended = lax.dot_general(
        grad_sum, w_full, (((1,), (1,)), ((), ())), preferred_element_type=jnp.float32
    ).astype(jnp.bfloat16)
    term = jnp.einsum("th,td->hd", attended, grad_sum, preferred_element_type=jnp.float32)
    shard = lax.psum_scatter(term.astype(jnp.bfloat16), "dp", scatter_dimension=0, tiled=True)
    weight_grad = lax.psum(shard, "seq").astype(jnp.float32) * (1.0 / lax.axis_size("dp"))
    grad_blocks = grad_attended.reshape(blocks, BLOCK, heads, HDIM)
    grad_shares = jnp.einsum(
        "jahe,jthe->jhat", grad_blocks, value_list, preferred_element_type=jnp.float32
    )
    centre = jnp.sum(shares * grad_shares, axis=-1, keepdims=True)
    grad_scores = (shares * (grad_shares - centre) * scale).astype(jnp.bfloat16)
    grad_query = jnp.einsum(
        "jhat,jthe->jahe", grad_scores, key_list, preferred_element_type=jnp.float32
    )
    grad_query = grad_query.astype(jnp.bfloat16).reshape(tokens, width)
    grad_keys = jnp.einsum(
        "jhat,jahe->jthe", grad_scores, query_blocks, preferred_element_type=jnp.float32
    )
    grad_values = jnp.einsum(
        "jhat,jahe->jthe", shares_low, grad_blocks, preferred_element_type=jnp.float32
    )
    grad_list = jnp.stack([grad_keys, grad_values]).reshape(2, blocks, listed, BLOCK, width)
    window_grad = jnp.pad(grad_list[:, :, 0], ((0, 0), (0, 2), (0, 0), (0, 0)))
    window_grad = window_grad + jnp.pad(grad_list[:, :, 1], ((0, 0), (1, 1), (0, 0), (0, 0)))
    window_grad = window_grad + jnp.pad(grad_list[:, :, 2], ((0, 0), (2, 0), (0, 0), (0, 0)))
    own_grad = window_grad[:, 1 : blocks + 1]
    rims = jnp.concatenate([window_grad[:, 0], window_grad[:, blocks + 1]], axis=1)
    arrived = padded(rims.astype(jnp.bfloat16), (("seq", 1),), BLOCK)
    from_left = arrived[:, :BLOCK].astype(jnp.float32)
    from_right = arrived[:, 3 * BLOCK :].astype(jnp.float32)
    own_grad = own_grad.at[:, 0].add(from_left).at[:, blocks - 1].add(from_right)
    glob_part = jnp.sum(grad_list[:, :, 3 : 3 + NG], axis=1)
    glob_total = lax.psum(glob_part.astype(jnp.bfloat16), "seq").astype(jnp.float32)
    own_grad = own_grad + jnp.einsum(
        "gq,cgax->cqax", owned.astype(jnp.float32), glob_total, precision=lax.Precision.HIGHEST
    )
    rand_part = grad_list[:, :, 3 + NG :].reshape(2, slots, BLOCK, width).astype(jnp.bfloat16)
    going_back = jnp.einsum(
        "sm,csax->cmax", recv_table, rand_part, preferred_element_type=jnp.float32
    ).astype(jnp.bfloat16)
    returned = lax.all_to_all(going_back, "seq", split_axis=1, concat_axis=1, tiled=True)
    own_grad = own_grad + jnp.einsum(
        "mq,cmax->cqax", send_table, returned, preferred_element_type=jnp.float32
    )
    grad_pairs = own_grad.astype(jnp.bfloat16).reshape(2, tokens, width)
    return (grad_query[None, None], grad_pairs[None, None], passed[None, None], weight_grad[None])


def solution(mesh):
    placed = (
        P("section", "dp", "seq", None),
        P("section", "dp", None, "seq", None),
        P("section", "dp", "seq", None),
        P("section", "dp", "seq", None),
        P("section", "dp", None),
        P("section", None),
        P("dp", None),
        P("dp", None, None),
    )
    return jax.shard_map(
        on_device,
        mesh=mesh,
        in_specs=placed,
        out_specs=(
            P("section", "dp", "seq", None),
            P("section", "dp", None, "seq", None),
            P("section", "dp", "seq", None),
            P("section", "dp", None),
        ),
        check_vma=False,
    )
```

profile of v0, /device:TPU:8, one launch (start us, length us, event | category | flops | bytes accessed | tf_op | source)
XLA Modules:
  0.0 461.0 jit_solution(1098913698455877146)
XLA Ops:
  19.1 4.3 copy.89
  23.3 6.7 %all-to-all-start = ((bf16[2,8,64,2048]{3,2,0,1:T(8,128)(2,1)}), bf16[2,8,64,2048]{3,2,0,1:T(8,128)(2,1)}, u32[]{:S(2)}, u32[]{:S(2)}) async-start(bf16[2,8,64,2048]{3,2,0,1:T(8,128)(2,1)} %copy.89), calls=%async_computation | async-start | bytes 8388608 | tf_op jit(solution)/shard_map/all_to_all | solution.py:101
  37.8 79.2 %collective-permute-done = bf16[2,64,2048]{2,1,0:T(8,128)(2,1)} collective-permute-done((bf16[2,64,2048]{2,1,0:T(8,128)(2,1)S(1)}, bf16[2,64,2048]{2,1,0:T(8,128)(2,1)}, u32[]{:S(2)}, u32[]{:S(2)}) %collective-permute-start) | collective-permute-done | bytes 524320 | tf_op jit(solution)/shard_map/ppermute | solution.py:27
  121.7 40.2 %all-reduce.11.cloned.1.call-done = (bf16[2,1,64,2048]{3,2,0,1:T(8,128)(2,1)}, bf16[2,1,64,2048]{3,2,0,1:T(8,128)(2,1)}) async-done(((bf16[2,1,64,2048]{3,2,0,1:T(8,128)(2,1)}, bf16[2,1,64,2048]{3,2,0,1:T(8,128)(2,1)}), (bf16[2,1,64,2048]{3,2,0,1:T(8,128)(2,1)}, bf16[2,1,64,2048]{3,2,0,1:T(8,128)(2,1)})) %all-reduce.11.cloned.1.call-update) | async-done | bytes 1048592 | tf_op jit(solution)/shard_map/psum | solution.py:16
  164.7 4.9 %convert_bitcast_fusion.1 = bf16[2,6,64,2048]{3,1,2,0:T(8,128)(2,1)S(1)} fusion(bf16[2,8,64,2048]{3,2,0,1:T(8,128)(2,1)} %all-to-all-done, s32[6]{0:T(128)S(1)} %fusion.139), kind=kOutput, calls=%fused_computation.35 | convolution fusion | flops 26738736 | bytes 7340056 | tf_op jit(solution)/shard_map/sm,cmax->csax/dot_general | solution.py:110
  186.8 5.0 %multiply_reduce_fusion.1 = (f32[128]{0:T(128)S(1)}, f32[128]{0:T(128)S(1)}, f32[128,2048]{1,0:T(8,128)S(1)}) fusion(f32[2048]{0:T(1024)S(1)} %bitcast.228, bf16[1,1,128,2048]{3,2,1,0:T(8,128)(2,1)S(1)} %copy-done.5, bf16[1,2048,2048]{2,1,0:T(8,128)(2,1)} %all-gather.3.cloned.1.call-done, bf16[16,8,16,128]{3,2,1,0:T(8,128)(2,1)S(1)} %bitcast.220, ...), kind=kOutput, calls=%fused_computation.90 | convolution fusion | flops 1075838720 | bytes 11019264 | tf_op jit(solution)/shard_map/dot_general | solution.py:141
  192.1 5.6 %convolution_convert_fusion = bf16[2048,2048]{1,0:T(8,128)(2,1)} fusion(bf16[128,2048]{1,0:T(8,128)(2,1)S(1)} %fusion.85, bf16[16,8,16,128]{3,2,1,0:T(8,128)(2,1)S(1)} %bitcast.221), kind=kOutput, calls=%fused_computation.14 | convolution fusion | flops 1077936128 | bytes 9437184 | tf_op jit(solution)/shard_map/th,td->hd/dot_general | solution.py:151
  197.8 6.4 %fusion.75 = bf16[16,8,16,128]{3,1,2,0:T(8,128)(2,1)S(1)} fusion(bf16[128,2048]{1,0:T(8,128)(2,1)S(1)} %fusion.85, bf16[1,2048,2048]{2,1,0:T(8,128)(2,1)} %all-gather.3.cloned.1.call-done), kind=kOutput, calls=%fused_computation.70 | convolution fusion | flops 1074003968 | bytes 9437184 | tf_op jit(solution)/shard_map/dot_general | solution.py:148
  204.3 4.1 fusion.26
  208.4 21.3 %convolution_bitcast_fusion.1 = f32[2,512,16,128]{3,1,2,0:T(8,128)} fusion(f32[2,16,64,512]{3,2,1,0:T(8,128)} %fusion.26, bf16[2,64,16,128]{3,2,1,0:T(8,128)(2,1)S(1)} %bitcast.223, f32[2,16,64,512]{3,2,1,0:T(8,128)} %copy-done.11, f32[2,16,64]{2,1,0:T(8,128)S(1)} %get-tuple-element.53), kind=kOutput, calls=%fused_computation.46 | convolution fusion | flops 275778048 | bytes 17309696 | tf_op jit(solution)/shard_map/jhat,jahe->jthe/dot_general | solution.py:164
  229.7 11.6 %copy.106 = f32[2,512,16,128]{3,2,1,0:T(8,128)} copy(f32[2,512,16,128]{3,1,2,0:T(8,128)} %convolution_bitcast_fusion.1) | data formatting | bytes 16777216 | tf_op jit(solution)/shard_map/jhat,jahe->jthe/transpose | solution.py:164
  241.3 9.3 %stack.33 = f32[1,2,8,64,2048]{4,3,2,1,0:T(8,128)} reshape(f32[2,512,16,128]{3,2,1,0:T(8,128)} %copy.106) | data formatting | bytes 16777216 | tf_op jit(solution)/shard_map/stack | solution.py:170
  250.6 6.8 %convolution_bitcast_fusion = f32[2,512,16,128]{1,3,2,0:T(8,128)} fusion(bf16[2,64,16,128]{3,2,1,0:T(8,128)(2,1)S(1)} %bitcast.225, f32[2,16,64,512]{3,2,1,0:T(8,128)} %copy-done.11, f32[2,16,64]{2,1,0:T(8,128)S(1)} %get-tuple-element.53), kind=kOutput, calls=%fused_computation.45 | convolution fusion | flops 270532608 | bytes 13115392 | tf_op jit(solution)/shard_map/jhat,jahe->jthe/dot_general | solution.py:167
  257.4 13.0 %reshape.304 = f32[1,2,8,64,2048]{3,2,4,1,0:T(8,128)} reshape(f32[2,512,16,128]{1,3,2,0:T(8,128)} %convolution_bitcast_fusion) | data formatting | bytes 16777216 | tf_op jit(solution)/shard_map/stack | solution.py:170
  270.4 12.9 %copy.110 = f32[1,2,8,64,2048]{4,3,0,1,2:T(8,128)} copy(f32[1,2,8,64,2048]{3,2,4,1,0:T(8,128)} %reshape.304) | data formatting | bytes 16777216 | tf_op jit(solution)/shard_map/stack | solution.py:170
  289.2 4.3 copy.117
  293.5 6.0 %all-to-all-start.1 = ((bf16[2,8,64,2048]{3,2,0,1:T(8,128)(2,1)}), bf16[2,8,64,2048]{3,2,0,1:T(8,128)(2,1)}, u32[]{:S(2)}, u32[]{:S(2)}) async-start(bf16[2,8,64,2048]{3,2,0,1:T(8,128)(2,1)} %copy.117), calls=%async_computation.1 | async-start | bytes 8388608 | tf_op jit(solution)/shard_map/all_to_all | solution.py:189
  308.3 4.0 collective-permute-start.2
  319.3 18.7 %fusion.67 = bf16[2,64,16,128]{3,1,2,0:T(8,128)(2,1)S(1)} fusion(bf16[2,512,16,128]{3,2,1,0:T(8,128)(2,1)} %bitcast.206, f32[2,16,64,512]{3,2,1,0:T(8,128)} %fusion.26, f32[2,16,64,512]{3,2,1,0:T(8,128)} %copy-done.11, f32[2,16,64]{2,1,0:T(8,128)S(1)} %get-tuple-element.53), kind=kOutput, calls=%fused_computation.68 | convolution fusion | flops 276040192 | bytes 13115392 | tf_op jit(solution)/shard_map/jhat,jthe->jahe/dot_general | solution.py:160
  341.1 63.4 %collective-permute-done.2 = bf16[2,64,2048]{2,1,0:T(8,128)(2,1)S(1)} collective-permute-done((bf16[2,64,2048]{2,1,0:T(8,128)(2,1)S(1)}, bf16[2,64,2048]{2,1,0:T(8,128)(2,1)S(1)}, u32[]{:S(2)}, u32[]{:S(2)}) %collective-permute-start.2) | collective-permute-done | bytes 524320 | tf_op jit(solution)/shard_map/ppermute | solution.py:27
  410.2 7.2 %scatter-add.9 = f32[2,2,64,2048]{3,1,2,0:T(2,128)S(1)} dynamic-update-slice(f32[2,2,64,2048]{3,1,2,0:T(2,128)S(1)} %copy.112, f32[2,1,64,2048]{3,1,2,0:T(1,128)S(1)} %copy_add_fusion, s32[]{:T(128)} %constant.133.clone.1, s32[]{:T(128)} %constant.132.clone.1, s32[]{:T(128)} %constant.133.clone.1, s32[]{:T(128)} %constant.133.clone.1) | dynamic-update-slice | bytes 2097156 | tf_op jit(solution)/shard_map/scatter-add | solution.py:179
  418.7 5.0 %fusion.34 = f32[2,2,64,2048]{3,1,2,0:T(2,128)S(1)} fusion(bf16[2,8,64,2048]{3,2,0,1:T(8,128)(2,1)} %all-to-all-done.1, bf16[8,1,2]{0,2,1:T(2,128)(2,1)S(1)} %copy.125), kind=kOutput, calls=%fused_computation.47 | convolution fusion | flops 8388608 | bytes 6291488 | tf_op jit(solution)/shard_map/mq,cmax->cqax/dot_general | solution.py:190
  423.7 19.7 %all-reduce.9.cloned.1.call-done = (bf16[2,2,64,2048]{3,1,2,0:T(2,128)(2,1)}, bf16[128,2048]{1,0:T(8,128)(2,1)}) async-done(((bf16[2,2,64,2048]{3,1,2,0:T(2,128)(2,1)}, bf16[128,2048]{1,0:T(8,128)(2,1)}), (bf16[2,2,64,2048]{3,1,2,0:T(2,128)(2,1)}, bf16[128,2048]{1,0:T(8,128)(2,1)})) %all-reduce.9.cloned.1.call-update) | async-done | bytes 1572880 | tf_op jit(solution)/shard_map/psum | solution.py:181
  445.5 4.3 fusion.39
  (108 shorter events, 79.4 us)
Async XLA Ops:
  8.0 3.4 copy-start.3
  8.0 153.9 %all-reduce.11.cloned.1.call-start = ((), (), s32[]{:S(2)}) async-start(), calls=%async_computation.6 | async-start | bytes 2097152 | tf_op jit(solution)/shard_map/psum | solution.py:16
  8.9 3.8 copy-start.10
  11.4 5.4 %copy-start.9 = (s32[1,16,3]{1,0,2:T(1,128)S(1)}, s32[1,16,3]{1,0,2:T(1,128)}, u32[]{:S(2)}) copy-start(s32[1,16,3]{1,0,2:T(1,128)} %param.19) | copy-start | bytes 580
  16.2 170.6 %all-gather.3.cloned.1.call-start = ((), (), s32[]{:S(2)}) async-start(), calls=%async_computation.4 | async-start | bytes 8912896 | tf_op jit(solution)/shard_map/all_gather | solution.py:140
  23.3 14.2 %copy-start.7 = (bf16[1,1,128,2048]{3,2,1,0:T(8,128)(2,1)S(1)}, bf16[1,1,128,2048]{3,2,1,0:T(8,128)(2,1)}, u32[]{:S(2)}) copy-start(bf16[1,1,128,2048]{3,2,1,0:T(8,128)(2,1)} %param.12) | copy-start | bytes 1572868
  23.3 141.4 %all-to-all-start = ((bf16[2,8,64,2048]{3,2,0,1:T(8,128)(2,1)}), bf16[2,8,64,2048]{3,2,0,1:T(8,128)(2,1)}, u32[]{:S(2)}, u32[]{:S(2)}) async-start(bf16[2,8,64,2048]{3,2,0,1:T(8,128)(2,1)} %copy.89), calls=%async_computation | async-start | bytes 8388608 | tf_op jit(solution)/shard_map/all_to_all | solution.py:101
  30.1 289.2 %reduce-scatter.2.cloned.1.call-start = ((), (), s32[]{:S(2)}) async-start(), calls=%async_computation.3 | async-start | bytes 8912896 | tf_op jit(solution)/shard_map/reduce_scatter | solution.py:152
  30.2 86.9 %collective-permute-start = (bf16[2,64,2048]{2,1,0:T(8,128)(2,1)S(1)}, bf16[2,64,2048]{2,1,0:T(8,128)(2,1)}, u32[]{:S(2)}, u32[]{:S(2)}) collective-permute-start(bf16[2,64,2048]{2,1,0:T(8,128)(2,1)S(1)} %get-tuple-element.47), channel_id=1, source_target_pairs={{0,2},{2,4},{4,6},{6,8},{8,10},{10,12},{12,14},{1,3},{3,5},{5,7},{... | collective-permute-start | bytes 1572872 | tf_op jit(solution)/shard_map/ppermute | solution.py:27
  33.6 83.5 %collective-permute-start.1 = (bf16[2,64,2048]{2,1,0:T(8,128)(2,1)S(1)}, bf16[2,64,2048]{2,1,0:T(8,128)(2,1)}, u32[]{:S(2)}, u32[]{:S(2)}) collective-permute-start(bf16[2,64,2048]{2,1,0:T(8,128)(2,1)S(1)} %get-tuple-element.48), channel_id=1, source_target_pairs={{2,0},{4,2},{6,4},{8,6},{10,8},{12,10},{14,12},{3,1},{5,3},{7,5},{... | collective-permute-start | bytes 1572872 | tf_op jit(solution)/shard_map/ppermute | solution.py:29
  178.6 5.1 %copy-start.1 = (bf16[128,8,16,128]{3,2,1,0:T(8,128)(2,1)}, bf16[128,8,16,128]{3,2,1,0:T(8,128)(2,1)S(1)}, u32[]{:S(2)}) copy-start(bf16[128,8,16,128]{3,2,1,0:T(8,128)(2,1)S(1)} %copy.136) | copy-start | bytes 12582916
  180.0 2.1 copy-start
  183.7 2.7 copy-start.11
  183.7 3.1 copy-start.5
  183.7 3.1 copy-start.6
  183.7 3.1 copy-start.8
  197.7 6.6 %copy-start.2 = (bf16[128,8,16,128]{3,2,1,0:T(8,128)(2,1)S(1)}, bf16[128,8,16,128]{3,2,1,0:T(8,128)(2,1)}, u32[]{:S(2)}) copy-start(bf16[128,8,16,128]{3,2,1,0:T(8,128)(2,1)} %copy-done.1) | copy-start | bytes 12582916
  293.5 125.3 %all-to-all-start.1 = ((bf16[2,8,64,2048]{3,2,0,1:T(8,128)(2,1)}), bf16[2,8,64,2048]{3,2,0,1:T(8,128)(2,1)}, u32[]{:S(2)}, u32[]{:S(2)}) async-start(bf16[2,8,64,2048]{3,2,0,1:T(8,128)(2,1)} %copy.117), calls=%async_computation.1 | async-start | bytes 8388608 | tf_op jit(solution)/shard_map/all_to_all | solution.py:189
  299.5 143.9 %all-reduce.9.cloned.1.call-start = ((), (), s32[]{:S(2)}) async-start(), calls=%async_computation.5 | async-start | bytes 3145728 | tf_op jit(solution)/shard_map/psum | solution.py:181
  299.5 108.1 %collective-permute-start.4 = (bf16[128,2048]{1,0:T(8,128)(2,1)S(1)}, bf16[128,2048]{1,0:T(8,128)(2,1)}, u32[]{:S(2)}, u32[]{:S(2)}) collective-permute-start(bf16[128,2048]{1,0:T(8,128)(2,1)S(1)} %fusion.85), channel_id=1, source_target_pairs={{1,0},{0,1},{3,2},{2,3},{5,4},{4,5},{7,6},{6,7},{9,8},{8,9},{11,10... | collective-permute-start | bytes 1572872 | tf_op jit(solution)/shard_map/ppermute | solution.py:39
  308.3 96.2 %collective-permute-start.2 = (bf16[2,64,2048]{2,1,0:T(8,128)(2,1)S(1)}, bf16[2,64,2048]{2,1,0:T(8,128)(2,1)S(1)}, u32[]{:S(2)}, u32[]{:S(2)}) collective-permute-start(bf16[2,64,2048]{2,1,0:T(8,128)(2,1)S(1)} %get-tuple-element.46), channel_id=1, source_target_pairs={{0,2},{2,4},{4,6},{6,8},{8,10},{10,12},{12,14},{1,3},{3,5},{5,7},{... | collective-permute-start | bytes 1572872 | tf_op jit(solution)/shard_map/ppermute | solution.py:27
  317.1 90.5 %collective-permute-start.3 = (bf16[2,64,2048]{2,1,0:T(8,128)(2,1)}, bf16[2,64,2048]{2,1,0:T(8,128)(2,1)}, u32[]{:S(2)}, u32[]{:S(2)}) collective-permute-start(bf16[2,64,2048]{2,1,0:T(8,128)(2,1)} %get-tuple-element.45), channel_id=1, source_target_pairs={{2,0},{4,2},{6,4},{8,6},{10,8},{12,10},{14,12},{3,1},{5,3},{7,5},{... | collective-permute-start | bytes 1572872 | tf_op jit(solution)/shard_map/ppermute | solution.py:29
  417.4 1.4 copy-start.4
Sparse Core Ops, SparseCore 0:
  16.3 145.5 all-reduce.10
  319.5 123.8 all-reduce.8
Sparse Core Ops, SparseCore 1:
  18.5 58.7 all-gather.2
  197.8 71.1 reduce-scatter.1
where the time goes:
time: 469 us; the launch traced here: 461 us
  waiting for transfers between devices  203 us (43%)
  matrix products  94.3 us (20%)
  local copies, waits for them, and re-layouts  90.8 us (19%)
  starting transfers between devices  28 us (6%)
  other arithmetic  26.9 us (6%)
  between operations  17.8 us (4%)
    ppermute x2, waiting for transfers between devices, padded(): lax.ppermute(tail, axis, [(i, (i + 1) % count) for i in range(ends)])  143 us
    psum x1, waiting for transfers between devices, from_root(): return lax.psum(block, axis)  40.2 us
    another operation x3, local copies, waits for them, and re-layouts, on_device(): jnp.stack([grad_keys, grad_values]).reshape(2, blocks, listed, BLOCK, width)  35.2 us
    dot_general x1, matrix products, on_device(): jnp.einsum('jhat,jahe->jthe', grad_scores, query_blocks, preferred_elemen...  21.3 us
    psum x1, waiting for transfers between devices, on_device(): lax.psum(glob_part.astype(jnp.bfloat16), 'seq').astype(jnp.float32)  19.7 us
    dot_general x1, matrix products, on_device(): jnp.einsum('jhat,jthe->jahe', grad_scores, key_list, preferred_element_ty...  18.7 us
    transpose x1, local copies, waits for them, and re-layouts, on_device(): jnp.einsum('jhat,jahe->jthe', grad_scores, query_blocks, preferred_elemen...  11.6 us
    unnamed x33, local copies, waits for them, and re-layouts  9.59 us
  transfers between devices with their start and end apart: 11, of which 4 were waited for; matrix products, arithmetic and copies ran while one was open for 40% of the time, Pallas kernels for 0%

commit v1 on v0

v1 whole, which is shorter than its diff:
```python
import functools
import math

import jax
import jax.numpy as jnp
from jax import lax
from jax.experimental import pallas as pl
from jax.experimental.pallas import tpu as pltpu
from jax.sharding import Mesh
from jax.sharding import PartitionSpec as P

HDIM = 128
BLOCK = 64
R = 3
NG = 2
QB = 2
N_SEQ = 8
NBLK = N_SEQ * QB
PAIR = 2 * HDIM
D = 2048
N_Z = 8
BATCH = 16
TOK = QB * BLOCK
LISTED = 3 + NG + R
SCALE = 1.0 / math.sqrt(HDIM)
NEG = -1e30
F32 = jnp.float32
BF16 = jnp.bfloat16
VMEM_LIMIT = 48 * 1024 * 1024


def dot(a, b, contract):
    return lax.dot_general(a, b, (contract, ((), ())), preferred_element_type=F32)


def diagonal(rows):
    zero = jnp.zeros((BLOCK, HDIM), rows.dtype)
    top = jnp.concatenate([rows[:, :HDIM], zero], axis=1)
    low = jnp.concatenate([zero, rows[:, HDIM:]], axis=1)
    return jnp.concatenate([top, low], axis=0)


def undiagonal(both):
    return jnp.concatenate([both[:BLOCK, :HDIM], both[BLOCK:, HDIM:]], axis=1)


def listed_blocks(j, glob_ref, rand_ref):
    window = [jnp.maximum(j - 1, 0), j, jnp.minimum(j + 1, NBLK - 1)]
    chosen = [glob_ref[g] for g in range(NG)]
    chosen += [rand_ref[j * R + r] for r in range(R)]
    return window + chosen


def take(got_ref, which, ids):
    return jnp.concatenate([got_ref[b // QB, which, b % QB] for b in ids], axis=0)


def share_columns(j, keys, query_diag):
    scores = dot(keys, query_diag, ((1,), (1,))) * SCALE
    first = jnp.where(j > 0, scores[:BLOCK], NEG)
    last = jnp.where(j < NBLK - 1, scores[2 * BLOCK : 3 * BLOCK], NEG)
    scores = jnp.concatenate(
        [first, scores[BLOCK : 2 * BLOCK], last, scores[3 * BLOCK :]], axis=0
    )
    top = jnp.max(scores, axis=0, keepdims=True)
    raised = jnp.exp(scores - top)
    total = jnp.sum(raised, axis=0, keepdims=True)
    return raised * (1.0 / total)


def forward_kernel(unroll, glob_ref, rand_ref, got_ref, att_ref):
    def one(j):
        ids = listed_blocks(j, glob_ref, rand_ref)
        keys = take(got_ref, 1, ids)
        values = take(got_ref, 2, ids)
        query_diag = diagonal(got_ref[j // QB, 0, j % QB])
        shares = share_columns(j, keys, query_diag).astype(BF16)
        att = dot(shares, values, ((0,), (0,)))
        att_ref[j // QB, j % QB] = undiagonal(att).astype(BF16)

    def step(g, carry):
        for u in range(unroll):
            one(g * unroll + u)
        return carry

    lax.fori_loop(0, NBLK // unroll, step, 0)


def backward_kernel(unroll, glob_ref, rand_ref, got_ref, grad_ref, out_ref, acc, glob_acc, rand_acc):
    acc[...] = jnp.zeros_like(acc)
    glob_acc[...] = jnp.zeros_like(glob_acc)
    rand_acc[...] = jnp.zeros_like(rand_acc)

    def one(j):
        ids = listed_blocks(j, glob_ref, rand_ref)
        keys = take(got_ref, 1, ids)
        values = take(got_ref, 2, ids)
        query_diag = diagonal(got_ref[j // QB, 0, j % QB])
        grad_diag = diagonal(grad_ref[j // QB, j % QB])
        shares = share_columns(j, keys, query_diag)
        grad_shares = dot(values, grad_diag, ((1,), (1,)))
        centre = jnp.sum(shares * grad_shares, axis=0, keepdims=True)
        grad_scores = (shares * (grad_shares - centre) * SCALE).astype(BF16)
        grad_query = dot(grad_scores, keys, ((0,), (0,)))
        out_ref[j // QB, 0, j % QB] = undiagonal(grad_query).astype(BF16)
        parts = (
            dot(grad_scores, query_diag, ((1,), (0,))),
            dot(shares.astype(BF16), grad_diag, ((1,), (0,))),
        )
        for which in range(2):
            part = parts[which]
            for n in range(3):
                acc[which, ids[n]] += part[n * BLOCK : (n + 1) * BLOCK]
            glob_acc[which] += part[3 * BLOCK : (3 + NG) * BLOCK]
            for n in range(3 + NG, LISTED):
                rand_acc[which, ids[n]] += part[n * BLOCK : (n + 1) * BLOCK]

    def step(g, carry):
        for u in range(unroll):
            one(g * unroll + u)
        return carry

    lax.fori_loop(0, NBLK // unroll, step, 0)
    for which in range(2):
        for g in range(NG):
            acc[which, glob_ref[g]] += glob_acc[which, g * BLOCK : (g + 1) * BLOCK]

    def finish(b, carry):
        for which in range(2):
            total = acc[which, b] + rand_acc[which, b]
            out_ref[b // QB, 1 + which, b % QB] = total.astype(BF16)
        return carry

    lax.fori_loop(0, NBLK, finish, 0)


def project_kernel(att_ref, w_hbm, resid_ref, up_ref, gain_ref, sum_ref, ga_ref, w_vmem, total, sems):
    copies = [
        pltpu.make_async_copy(
            w_hbm.at[pl.ds(s * PAIR, PAIR)], w_vmem.at[pl.ds(s * PAIR, PAIR)], sems.at[s]
        )
        for s in range(N_SEQ)
    ]
    for copy in copies:
        copy.start()
    total[...] = resid_ref[...].astype(F32)
    for s in range(N_SEQ):
        copies[s].wait()
        total[...] += dot(att_ref[s], w_vmem[s * PAIR : (s + 1) * PAIR], ((1,), (0,)))
    summed = total[...]
    inverse = lax.rsqrt(jnp.mean(summed * summed, axis=-1, keepdims=True) + 1e-06)
    scaled = up_ref[...].astype(F32) * gain_ref[...]
    inner = jnp.mean(scaled * summed, axis=-1, keepdims=True)
    grad_sum = (inverse * scaled - summed * (inverse * inverse * inverse * inner)).astype(BF16)
    sum_ref[...] = grad_sum
    for s in range(N_SEQ):
        part = dot(grad_sum, w_vmem[s * PAIR : (s + 1) * PAIR], ((1,), (1,)))
        ga_ref[s] = part.astype(BF16)


def term_kernel(own_ref, other_ref, own_sum_ref, other_sum_ref, out_ref):
    for n in range(N_Z):
        part = dot(own_ref[n], own_sum_ref[...], ((0,), (0,)))
        part += dot(other_ref[n], other_sum_ref[...], ((0,), (0,)))
        out_ref[n] = part.astype(BF16)


def split_kernel(rows_ref, after_ref, out_ref):
    for s in range(N_SEQ):
        out_ref[s] = rows_ref[:, s * PAIR : (s + 1) * PAIR]


def spread_kernel(parts_ref, out_ref):
    total = parts_ref[0].astype(F32)
    for n in range(1, N_SEQ):
        total += parts_ref[n].astype(F32)
    total = total.astype(BF16)
    for s in range(N_SEQ):
        out_ref[s] = total


def average_kernel(pieces_ref, out_ref):
    for s in range(N_SEQ):
        out_ref[:, s * PAIR : (s + 1) * PAIR] = pieces_ref[s].astype(F32) * (1.0 / BATCH)


def vmem():
    return pl.BlockSpec(memory_space=pltpu.VMEM)


def anywhere():
    return pl.BlockSpec(memory_space=pl.ANY)


def smem():
    return pl.BlockSpec(memory_space=pltpu.SMEM)


def call(kernel, name, out_shape, in_specs, out_specs, scratch=(), flops=0, moved=0):
    return pl.pallas_call(
        kernel,
        out_shape=out_shape,
        in_specs=in_specs,
        out_specs=out_specs,
        scratch_shapes=list(scratch),
        compiler_params=pltpu.CompilerParams(vmem_limit_bytes=VMEM_LIMIT),
        cost_estimate=pl.CostEstimate(flops=flops, bytes_accessed=moved, transcendentals=0),
        name=name,
    )


def exchange(chunks):
    return lax.all_to_all(chunks, "seq", 0, 0, tiled=True)


def on_device(queries, key_values, resid, upstream, w_out, gain, global_ids, random_ids):
    core = lax.axis_index("core")
    swap = [(0, 1), (1, 0)]
    glob_ids = global_ids[0]
    rand_ids = random_ids[0].reshape(NBLK * R)

    with jax.named_scope("gather_w"):
        w_full = lax.all_gather(w_out[0], ("z", "core"), axis=0, tiled=True)

    with jax.named_scope("to_heads"):
        packed = jnp.concatenate([queries[0], key_values[0, 0]], axis=0)
        packed = packed.reshape(3, TOK, N_SEQ, PAIR).transpose(2, 0, 1, 3)
        got = exchange(packed).reshape(N_SEQ, 3, QB, BLOCK, PAIR)

    with jax.named_scope("forward"):
        att = call(
            functools.partial(forward_kernel, 8),
            "attention_forward",
            jax.ShapeDtypeStruct((N_SEQ, QB, BLOCK, PAIR), BF16),
            [smem(), smem(), vmem()],
            vmem(),
            flops=1_000_000_000,
            moved=2_000_000,
        )(glob_ids, rand_ids, got)

    with jax.named_scope("to_tokens"):
        att = exchange(att.reshape(N_SEQ, TOK, PAIR))

    with jax.named_scope("project"):
        grad_sum, grad_att = call(
            project_kernel,
            "project",
            (
                jax.ShapeDtypeStruct((TOK, D), BF16),
                jax.ShapeDtypeStruct((N_SEQ, TOK, PAIR), BF16),
            ),
            [vmem(), anywhere(), vmem(), vmem(), vmem()],
            (vmem(), vmem()),
            [
                pltpu.VMEM((D, D), BF16),
                pltpu.VMEM((TOK, D), F32),
                pltpu.SemaphoreType.DMA((N_SEQ,)),
            ],
            flops=2_000_000_000,
            moved=10_000_000,
        )(att, w_full, resid[0, 0], upstream[0, 0], gain)

    with jax.named_scope("grad_to_heads"):
        grad_got = exchange(grad_att).reshape(N_SEQ, QB, BLOCK, PAIR)

    with jax.named_scope("weight_grad"):
        halves = att.reshape(N_SEQ, TOK, 2, HDIM)
        own = jnp.where(core == 0, halves[:, :, 0], halves[:, :, 1])
        given = jnp.where(core == 0, halves[:, :, 1], halves[:, :, 0])
        other = lax.ppermute(given, "core", swap)
        other_sum = lax.ppermute(grad_sum, "core", swap)
        term = call(
            term_kernel,
            "weight_term",
            jax.ShapeDtypeStruct((N_Z, HDIM, D), BF16),
            [vmem()] * 4,
            vmem(),
            flops=1_000_000_000,
            moved=6_000_000,
        )(own, other, grad_sum, other_sum)
        shard = lax.psum_scatter(
            term.reshape(N_Z * HDIM, D), "z", scatter_dimension=0, tiled=True
        )

    with jax.named_scope("passed"):
        passed = lax.ppermute(grad_sum, "section", swap)

    with jax.named_scope("backward"):
        grads = call(
            functools.partial(backward_kernel, 8),
            "attention_backward",
            jax.ShapeDtypeStruct((N_SEQ, 3, QB, BLOCK, PAIR), BF16),
            [smem(), smem(), vmem(), vmem()],
            vmem(),
            [
                pltpu.VMEM((2, NBLK, BLOCK, PAIR), F32),
                pltpu.VMEM((2, NG * BLOCK, PAIR), F32),
                pltpu.VMEM((2, NBLK, BLOCK, PAIR), F32),
            ],
            flops=3_000_000_000,
            moved=4_000_000,
        )(glob_ids, rand_ids, got, grad_got)

    with jax.named_scope("grads_to_tokens"):
        back = exchange(grads.reshape(N_SEQ, 3, TOK, PAIR))

    with jax.named_scope("weight_grad"):
        pieces = call(
            split_kernel,
            "weight_split",
            jax.ShapeDtypeStruct((N_SEQ, HDIM, PAIR), BF16),
            [vmem(), anywhere()],
            vmem(),
            flops=1_000_000,
            moved=1_000_000,
        )(shard, back)
        spread = call(
            spread_kernel,
            "weight_sum",
            jax.ShapeDtypeStruct((N_SEQ, HDIM, PAIR), BF16),
            [vmem()],
            vmem(),
            flops=1_000_000,
            moved=1_000_000,
        )(exchange(pieces))
        weight_grad = call(
            average_kernel,
            "average",
            jax.ShapeDtypeStruct((HDIM, D), F32),
            [vmem()],
            vmem(),
            flops=1_000_000,
            moved=1_500_000,
        )(exchange(spread))

    with jax.named_scope("unpack"):
        back = back.transpose(1, 2, 0, 3).reshape(3, TOK, D)
    return (back[None, :1].reshape(1, 1, TOK, D), back[None, None, 1:], passed[None, None], weight_grad[None])


def solution(mesh):
    fine = Mesh(mesh.devices.reshape(8, 2, 8, 2), ("z", "core", "seq", "section"))
    dp = ("z", "core")
    tokens = P("section", dp, "seq", None)
    pairs = P("section", dp, None, "seq", None)
    rows = P("section", dp, None)
    return jax.shard_map(
        on_device,
        mesh=fine,
        in_specs=(
            tokens,
            pairs,
            tokens,
            tokens,
            rows,
            P("section", None),
            P(dp, None),
            P(dp, None, None),
        ),
        out_specs=(tokens, pairs, tokens, rows),
        check_vma=False,
    )
```

time: 469 us -> 186 us (0.40); the launches traced: 461 us -> 185 us
  waiting for transfers between devices: 203 us -> 58.3 us
  matrix products: 94.3 us -> 0 us
  local copies, waits for them, and re-layouts: 90.8 us -> 16.8 us
  blocking collectives: 0 us -> 38.3 us
  Pallas kernels: 0 us -> 32.3 us
  other arithmetic: 26.9 us -> 1.37 us
    ppermute x5 -> x3, waiting for transfers between devices: 143 us -> 12.2 us  [the longest x1 10.9 us: on_device(): passed = lax.ppermute(grad_sum, 'section', swap)]
    dot_general x17 -> x0, matrix products: 94.3 us -> none  [the longest x1 21.3 us: on_device(): jnp.einsum('jhat,jahe->jthe', grad_scores, query_blocks, preferred_elemen...]
    psum x2 -> x0, waiting for transfers between devices: 59.9 us -> none  [the longest x1 40.2 us: from_root(): return lax.psum(block, axis)]
    all_to_all x0 -> x2, blocking collectives: none -> 38.3 us  [exchange(): return lax.all_to_all(chunks, 'seq', 0, 0, tiled=True)]
    all_to_all x2 -> x4, waiting for transfers between devices: 0.01 us -> 36.7 us  [exchange(): return lax.all_to_all(chunks, 'seq', 0, 0, tiled=True)]
    another operation x6 -> x1, local copies, waits for them, and re-layouts: 36.4 us -> 0.09 us  [on_device(): rand_ids = random_ids[0].reshape(NBLK * R)]
    pallas_call x0 -> x7, Pallas kernels: none -> 32.3 us  [the longest x1 10.9 us: on_device(): call(functools.partial(backward_kernel, 8), 'attention_backward', jax.Sha...]
    ppermute x5 -> x3, starting transfers between devices: 15.1 us -> 2.71 us  [the longest x1 2.11 us: on_device(): passed = lax.ppermute(grad_sum, 'section', swap)]
  transfers between devices with their start and end apart: 11 -> 9, of which waited for: 4 -> 7; matrix products, arithmetic and copies ran while one was open for 40% -> 5% of each run, Pallas kernels for 0% -> 11%
where the time goes in v1:
time: 186 us; the launch traced here: 185 us
  waiting for transfers between devices  58.3 us (31%)
  blocking collectives  38.3 us (21%)
  Pallas kernels  32.3 us (17%)
  starting transfers between devices  23.9 us (13%)
  local copies, waits for them, and re-layouts  16.8 us (9%)
  between operations  14.2 us (8%)
    all_to_all x2, blocking collectives, exchange(): return lax.all_to_all(chunks, 'seq', 0, 0, tiled=True)  38.3 us
    all_to_all x4, waiting for transfers between devices, exchange(): return lax.all_to_all(chunks, 'seq', 0, 0, tiled=True)  36.7 us
    all_to_all x4, starting transfers between devices, exchange(): return lax.all_to_all(chunks, 'seq', 0, 0, tiled=True)  21.2 us
    unnamed x36, local copies, waits for them, and re-layouts  12.4 us
    ppermute x1, waiting for transfers between devices, on_device(): passed = lax.ppermute(grad_sum, 'section', swap)  10.9 us
    pallas_call x1, Pallas kernels, on_device(): call(functools.partial(backward_kernel, 8), 'attention_backward', jax.Sha...  10.9 us
    pallas_call x1, Pallas kernels, on_device(): call(functools.partial(forward_kernel, 8), 'attention_forward', jax.Shape...  8.47 us
    pallas_call x1, Pallas kernels, on_device(): call(project_kernel, 'project', (jax.ShapeDtypeStruct((TOK, D), BF16), ja...  6.85 us
  transfers between devices with their start and end apart: 9, of which 7 were waited for; matrix products, arithmetic and copies ran while one was open for 5% of the time, Pallas kernels for 11%

profile of v1, /device:TPU:8, one launch (start us, length us, event | category | flops | bytes accessed | tf_op | source)
XLA Modules:
  0.0 185.1 jit_solution(10498079399333441123)
XLA Ops:
  7.9 1.5 copy.28
  10.7 1.3 maximum_bitcast_fusion
  12.0 5.9 %all-to-all-start = ((bf16[8,3,128,256]{3,2,1,0:T(8,128)(2,1)}), bf16[8,3,128,256]{3,2,1,0:T(8,128)(2,1)S(1)}, u32[]{:S(2)}, u32[]{:S(2)}) async-start(bf16[8,3,128,256]{3,2,1,0:T(8,128)(2,1)} %maximum_bitcast_fusion), calls=%async_computation | async-start | bytes 3145728 | tf_op jit(solution)/shard_map/to_heads/all_to_all | solution.py:213
  18.1 21.5 %all-to-all-done = bf16[8,3,128,256]{3,2,1,0:T(8,128)(2,1)S(1)} async-done(((bf16[8,3,128,256]{3,2,1,0:T(8,128)(2,1)}), bf16[8,3,128,256]{3,2,1,0:T(8,128)(2,1)S(1)}, u32[]{:S(2)}, u32[]{:S(2)}) %all-to-all-start) | async-done | bytes 1572896 | tf_op jit(solution)/shard_map/to_heads/all_to_all | solution.py:213
  39.6 8.5 %attention_forward.1 = bf16[8,2,64,256]{3,2,1,0:T(8,128)(2,1)S(1)} custom-call(s32[2]{0:T(128)S(1)} %bitcast.41, s32[48]{0:T(128)S(1)} %reshape_squeeze.3.rand_ref, bf16[8,3,2,64,256]{4,3,2,1,0:T(8,128)(2,1)S(1)} %bitcast.34), custom_call_target="tpu_custom_call" | custom-call | flops 1000000000 | bytes 2000000 | tf_op jit(solution)/shard_map/forward/attention_forward/pallas_call | solution.py:231
  48.9 5.6 %all-to-all-start.1 = ((bf16[8,128,256]{2,1,0:T(8,128)(2,1)}), bf16[8,128,256]{2,1,0:T(8,128)(2,1)S(1)}, u32[]{:S(2)}, u32[]{:S(2)}) async-start(bf16[8,128,256]{2,1,0:T(8,128)(2,1)} %bitcast.39), calls=%async_computation.1 | async-start | bytes 1048576 | tf_op jit(solution)/shard_map/to_tokens/all_to_all | solution.py:213
  54.5 8.3 %all-to-all-done.1.att_ref = bf16[8,128,256]{2,1,0:T(8,128)(2,1)S(1)} async-done(((bf16[8,128,256]{2,1,0:T(8,128)(2,1)}), bf16[8,128,256]{2,1,0:T(8,128)(2,1)S(1)}, u32[]{:S(2)}, u32[]{:S(2)}) %all-to-all-start.1) | async-done | bytes 524320 | tf_op jit(solution)/shard_map/to_tokens/all_to_all | solution.py:213
  63.8 4.9 %all-gather.3.cloned.1.call-done = bf16[1,2048,2048]{2,1,0:T(8,128)(2,1)} async-done(((bf16[1,128,2048]{2,1,0:T(8,128)(2,1)}), bf16[1,2048,2048]{2,1,0:T(8,128)(2,1)}) %all-gather.3.cloned.1.call-update) | async-done | bytes 8388624 | tf_op jit(solution)/shard_map/gather_w/all_gather | solution.py:223
  68.7 6.8 %project.1 = (bf16[128,2048]{1,0:T(8,128)(2,1)}, bf16[8,128,256]{2,1,0:T(8,128)(2,1)S(1)}) custom-call(bf16[8,128,256]{2,1,0:T(8,128)(2,1)S(1)} %all-to-all-done.1.att_ref, bf16[2048,2048]{1,0:T(8,128)(2,1)} %bitcast.43, bf16[128,2048]{1,0:T(8,128)(2,1)S(1)} %bitcast.37, bf16[128,2048]{1,0:T(8,128)(2,1)S(1)} %bitcast.38, f32[1,2048]{1,0:T(1,128)S(1)} %copy-done.7), custom_call_target="tpu_custom_call" | custom-call | flops 2000000000 | bytes 10000000 | tf_op jit(solution)/shard_map/project/project/pallas_call | solution.py:245
  77.4 1.3 collective-permute-done.1.other_ref
  78.7 3.4 %weight_term.1 = bf16[8,128,2048]{2,1,0:T(8,128)(2,1)S(1)} custom-call(bf16[8,128,128]{2,1,0:T(8,128)(2,1)S(1)} %get-tuple-element.13.own_ref, bf16[8,128,128]{2,1,0:T(8,128)(2,1)S(1)} %collective-permute-done.1.other_ref, bf16[128,2048]{1,0:T(8,128)(2,1)} %get-tuple-element.7.own_sum_ref, bf16[128,2048]{1,0:T(8,128)(2,1)S(1)} %collective-permute-done.2.other_sum_ref), custom_call_target="tpu_custom_call" | custom-call | flops 1000000000 | bytes 6000000 | tf_op jit(solution)/shard_map/weight_grad/weight_term/pallas_call | solution.py:272
  82.1 2.0 %copy-done = bf16[8,128,2048]{2,1,0:T(8,128)(2,1)} copy-done((bf16[8,128,2048]{2,1,0:T(8,128)(2,1)}, bf16[8,128,2048]{2,1,0:T(8,128)(2,1)S(1)}, u32[]{:S(2)}) %copy-start) | copy-done | bytes 4194328
  85.1 14.8 %all_to_all.30 = bf16[8,128,256]{2,1,0:T(8,128)(2,1)S(1)} all-to-all(bf16[8,128,256]{2,1,0:T(8,128)(2,1)S(1)} %copy-done.5), channel_id=1, replica_groups=mesh['z'=8,'core'=2,'seq'=8,'section'=2] {'seq'}, dimensions={0} | all-to-all | bytes 1048576 | tf_op jit(solution)/shard_map/grad_to_heads/all_to_all | solution.py:213
  99.9 10.9 %attention_backward.1 = bf16[8,3,2,64,256]{4,3,2,1,0:T(8,128)(2,1)S(1)} custom-call(s32[2]{0:T(128)S(1)} %bitcast.42, s32[48]{0:T(128)S(1)} %reshape_squeeze.3.rand_ref, bf16[8,3,2,64,256]{4,3,2,1,0:T(8,128)(2,1)S(1)} %bitcast.35, bf16[8,2,64,256]{3,2,1,0:T(8,128)(2,1)S(1)} %bitcast.40), custom_call_target="tpu_custom_call" | custom-call | flops 3000000000 | bytes 4000000 | tf_op jit(solution)/shard_map/backward/attention_backward/pallas_call | solution.py:289
  110.8 23.4 %all_to_all.31.after_ref = bf16[8,3,128,256]{3,2,1,0:T(8,128)(2,1)S(1)} all-to-all(bf16[8,3,128,256]{3,2,1,0:T(8,128)(2,1)S(1)} %bitcast.36), channel_id=1, replica_groups=mesh['z'=8,'core'=2,'seq'=8,'section'=2] {'seq'}, dimensions={0} | all-to-all | bytes 3145728 | tf_op jit(solution)/shard_map/grads_to_tokens/all_to_all | solution.py:213
  134.2 3.8 %reduce-scatter.2.cloned.1.call-done.rows_ref = bf16[128,2048]{1,0:T(8,128)(2,1)} async-done(((bf16[1024,2048]{1,0:T(8,128)(2,1)}), bf16[128,2048]{1,0:T(8,128)(2,1)}) %reduce-scatter.2.cloned.1.call-update) | async-done | bytes 524304 | tf_op jit(solution)/shard_map/weight_grad/reduce_scatter | solution.py:281
  139.9 5.7 %all-to-all-start.4 = ((bf16[8,128,256]{2,1,0:T(8,128)(2,1)}), bf16[8,128,256]{2,1,0:T(8,128)(2,1)S(1)}, u32[]{:S(2)}, u32[]{:S(2)}) async-start(bf16[8,128,256]{2,1,0:T(8,128)(2,1)} %weight_split.1), calls=%async_computation.5 | async-start | bytes 1048576 | tf_op jit(solution)/shard_map/weight_grad/all_to_all | solution.py:213
  145.7 2.1 %collective-permute-start = (bf16[128,2048]{1,0:T(8,128)(2,1)}, bf16[128,2048]{1,0:T(8,128)(2,1)S(1)}, u32[]{:S(2)}, u32[]{:S(2)}) collective-permute-start(bf16[128,2048]{1,0:T(8,128)(2,1)} %get-tuple-element.7.own_sum_ref), channel_id=1, source_target_pairs={{0,1},{1,0},{2,3},{3,2},{4,5},{5,4},{6,7},{7,6},{8,9},{9,8},{10,11... | collective-permute-start | bytes 1572872 | tf_op jit(solution)/shard_map/passed/ppermute | solution.py:286
  147.8 6.9 %all-to-all-done.4.parts_ref = bf16[8,128,256]{2,1,0:T(8,128)(2,1)S(1)} async-done(((bf16[8,128,256]{2,1,0:T(8,128)(2,1)}), bf16[8,128,256]{2,1,0:T(8,128)(2,1)S(1)}, u32[]{:S(2)}, u32[]{:S(2)}) %all-to-all-start.4) | async-done | bytes 524320 | tf_op jit(solution)/shard_map/weight_grad/all_to_all | solution.py:213
  155.5 4.0 %all-to-all-start.5 = ((bf16[8,128,256]{2,1,0:T(8,128)(2,1)}), bf16[8,128,256]{2,1,0:T(8,128)(2,1)S(1)}, u32[]{:S(2)}, u32[]{:S(2)}) async-start(bf16[8,128,256]{2,1,0:T(8,128)(2,1)} %weight_sum.1), calls=%async_computation.6 | async-start | bytes 1048576 | tf_op jit(solution)/shard_map/weight_grad/all_to_all | solution.py:213
  159.5 10.9 %collective-permute-done = bf16[128,2048]{1,0:T(8,128)(2,1)S(1)} collective-permute-done((bf16[128,2048]{1,0:T(8,128)(2,1)}, bf16[128,2048]{1,0:T(8,128)(2,1)S(1)}, u32[]{:S(2)}, u32[]{:S(2)}) %collective-permute-start) | collective-permute-done | bytes 524320 | tf_op jit(solution)/shard_map/passed/ppermute | solution.py:286
  172.1 1.3 copy.18
  175.1 1.3 copy.24
  176.4 1.0 average.1
  (52 shorter events, 13.7 us)
Async XLA Ops:
  7.2 61.5 %all-gather.3.cloned.1.call-start = ((), (), s32[]{:S(2)}) async-start(), calls=%async_computation.8 | async-start | bytes 8912896 | tf_op jit(solution)/shard_map/gather_w/all_gather | solution.py:223
  9.4 1.0 copy-start.10
  12.0 5.9 %copy-start.13 = (s32[1,16,3]{1,0,2:T(1,128)S(1)}, s32[1,16,3]{1,0,2:T(1,128)}, u32[]{:S(2)}) copy-start(s32[1,16,3]{1,0,2:T(1,128)} %param.15) | copy-start | bytes 580
  12.0 27.6 %copy-start.8 = (s32[1,2]{1,0:T(1,128)S(1)}, s32[1,2]{1,0:T(1,128)}, u32[]{:S(2)}) copy-start(s32[1,2]{1,0:T(1,128)} %param.14) | copy-start | bytes 28
  12.0 27.5 %all-to-all-start = ((bf16[8,3,128,256]{3,2,1,0:T(8,128)(2,1)}), bf16[8,3,128,256]{3,2,1,0:T(8,128)(2,1)S(1)}, u32[]{:S(2)}, u32[]{:S(2)}) async-start(bf16[8,3,128,256]{3,2,1,0:T(8,128)(2,1)} %maximum_bitcast_fusion), calls=%async_computation | async-start | bytes 3145728 | tf_op jit(solution)/shard_map/to_heads/all_to_all | solution.py:213
  48.1 0.8 copy-start.6
  48.9 19.8 %copy-start.1 = (bf16[1,1,128,2048]{3,2,1,0:T(8,128)(2,1)S(1)}, bf16[1,1,128,2048]{3,2,1,0:T(8,128)(2,1)}, u32[]{:S(2)}) copy-start(bf16[1,1,128,2048]{3,2,1,0:T(8,128)(2,1)} %param.10) | copy-start | bytes 1572868
  48.9 19.8 %copy-start.2 = (bf16[1,1,128,2048]{3,2,1,0:T(8,128)(2,1)S(1)}, bf16[1,1,128,2048]{3,2,1,0:T(8,128)(2,1)}, u32[]{:S(2)}) copy-start(bf16[1,1,128,2048]{3,2,1,0:T(8,128)(2,1)} %param.11) | copy-start | bytes 1572868
  48.9 19.8 %copy-start.7 = (f32[1,2048]{1,0:T(1,128)S(1)}, f32[1,2048]{1,0:T(1,128)}, u32[]{:S(2)}) copy-start(f32[1,2048]{1,0:T(1,128)} %gain_ref.1) | copy-start | bytes 24580
  48.9 13.9 %all-to-all-start.1 = ((bf16[8,128,256]{2,1,0:T(8,128)(2,1)}), bf16[8,128,256]{2,1,0:T(8,128)(2,1)S(1)}, u32[]{:S(2)}, u32[]{:S(2)}) async-start(bf16[8,128,256]{2,1,0:T(8,128)(2,1)} %bitcast.39), calls=%async_computation.1 | async-start | bytes 1048576 | tf_op jit(solution)/shard_map/to_tokens/all_to_all | solution.py:213
  54.5 83.6 %reduce-scatter.2.cloned.1.call-start = ((), (), s32[]{:S(2)}) async-start(), calls=%async_computation.7 | async-start | bytes 4718592 | tf_op jit(solution)/shard_map/weight_grad/reduce_scatter | solution.py:281
  68.7 7.9 %copy-start.9 = (bf16[8,128,256]{1,2,0:T(8,128)(2,1)S(1)}, bf16[8,128,256]{1,2,0:T(8,128)(2,1)}, u32[]{:S(2)}) copy-start(bf16[8,128,256]{1,2,0:T(8,128)(2,1)} %copy.20) | copy-start | bytes 1572868
  75.5 0.8 copy-start.4
  76.3 2.3 %collective-permute-start.2 = (bf16[128,2048]{1,0:T(8,128)(2,1)}, bf16[128,2048]{1,0:T(8,128)(2,1)S(1)}, u32[]{:S(2)}, u32[]{:S(2)}) collective-permute-start(bf16[128,2048]{1,0:T(8,128)(2,1)} %get-tuple-element.7.own_sum_ref), channel_id=1, source_target_pairs={{0,16},{16,0},{1,17},{17,1},{2,18},{18,2},{3,19},{19,3},{4,20},{20... | collective-permute-start | bytes 1572872 | tf_op jit(solution)/shard_map/weight_grad/ppermute | solution.py:271
  77.0 1.6 collective-permute-start.1
  82.1 2.0 %copy-start = (bf16[8,128,2048]{2,1,0:T(8,128)(2,1)}, bf16[8,128,2048]{2,1,0:T(8,128)(2,1)S(1)}, u32[]{:S(2)}) copy-start(bf16[8,128,2048]{2,1,0:T(8,128)(2,1)S(1)} %weight_term.1) | copy-start | bytes 12582916
  84.0 1.0 copy-start.5
  138.1 1.0 copy-start.3
  139.9 14.7 %all-to-all-start.4 = ((bf16[8,128,256]{2,1,0:T(8,128)(2,1)}), bf16[8,128,256]{2,1,0:T(8,128)(2,1)S(1)}, u32[]{:S(2)}, u32[]{:S(2)}) async-start(bf16[8,128,256]{2,1,0:T(8,128)(2,1)} %weight_split.1), calls=%async_computation.5 | async-start | bytes 1048576 | tf_op jit(solution)/shard_map/weight_grad/all_to_all | solution.py:213
  145.7 24.7 %collective-permute-start = (bf16[128,2048]{1,0:T(8,128)(2,1)}, bf16[128,2048]{1,0:T(8,128)(2,1)S(1)}, u32[]{:S(2)}, u32[]{:S(2)}) collective-permute-start(bf16[128,2048]{1,0:T(8,128)(2,1)} %get-tuple-element.7.own_sum_ref), channel_id=1, source_target_pairs={{0,1},{1,0},{2,3},{3,2},{4,5},{5,4},{6,7},{7,6},{8,9},{9,8},{10,11... | collective-permute-start | bytes 1572872 | tf_op jit(solution)/shard_map/passed/ppermute | solution.py:286
  155.5 20.9 %all-to-all-start.5 = ((bf16[8,128,256]{2,1,0:T(8,128)(2,1)}), bf16[8,128,256]{2,1,0:T(8,128)(2,1)S(1)}, u32[]{:S(2)}, u32[]{:S(2)}) async-start(bf16[8,128,256]{2,1,0:T(8,128)(2,1)} %weight_sum.1), calls=%async_computation.6 | async-start | bytes 1048576 | tf_op jit(solution)/shard_map/weight_grad/all_to_all | solution.py:213
  170.4 0.8 copy-start.11
  175.1 2.4 %copy-start.12 = (bf16[128,2048]{1,0:T(8,128)(2,1)S(1)}, bf16[128,2048]{1,0:T(8,128)(2,1)}, u32[]{:S(2)}) copy-start(bf16[128,2048]{1,0:T(8,128)(2,1)} %copy-done.11) | copy-start | bytes 1572868
Sparse Core Ops, SparseCore 0:
  9.8 58.7 all-gather.2
  84.2 53.8 reduce-scatter.1

commit v2 on v1

--- a/solution.py
+++ b/solution.py
@@ -158,16 +158,41 @@
         ga_ref[s] = part.astype(BF16)
 
 
-def term_kernel(own_ref, other_ref, own_sum_ref, other_sum_ref, out_ref):
+def term_kernel(core_ref, own_ref, other_ref, own_sum_ref, other_sum_ref, out_hbm, held, sems):
+    columns = pl.ds(pl.multiple_of(core_ref[0] * HDIM, HDIM), HDIM)
+    copies = []
     for n in range(N_Z):
-        part = dot(own_ref[n], own_sum_ref[...], ((0,), (0,)))
-        part += dot(other_ref[n], other_sum_ref[...], ((0,), (0,)))
-        out_ref[n] = part.astype(BF16)
-
-
-def split_kernel(rows_ref, after_ref, out_ref):
+        part = dot(own_ref[n, :, columns], own_sum_ref[...], ((0,), (0,)))
+        part += dot(other_ref[n, :, columns], other_sum_ref[...], ((0,), (0,)))
+        part = part.astype(BF16)
+        for s in range(N_SEQ):
+            held[n, s] = part[:, s * PAIR : (s + 1) * PAIR]
+        copies.append(pltpu.make_async_copy(held.at[n], out_hbm.at[n], sems.at[n]))
+        copies[-1].start()
+    for copy in copies:
+        copy.wait()
+
+
+def touch_kernel(rows_hbm, after_hbm, out_hbm, sem):
+    copy = pltpu.make_async_copy(rows_hbm, out_hbm, sem)
+    copy.start()
+    copy.wait()
+
+
+def unpack_kernel(back_hbm, query_hbm, pairs_hbm, sems):
+    copies = []
     for s in range(N_SEQ):
-        out_ref[s] = rows_ref[:, s * PAIR : (s + 1) * PAIR]
+        at = pl.ds(s * PAIR, PAIR)
+        copies += [
+            pltpu.make_async_copy(back_hbm.at[s, 0], query_hbm.at[:, at], sems.at[s, 0]),
+            pltpu.make_async_copy(
+                back_hbm.at[s, pl.ds(1, 2)], pairs_hbm.at[:, :, at], sems.at[s, 1]
+            ),
+        ]
+    for copy in copies:
+        copy.start()
+    for copy in copies:
+        copy.wait()
 
 
 def spread_kernel(parts_ref, out_ref):
@@ -264,26 +289,35 @@
         grad_got = exchange(grad_att).reshape(N_SEQ, QB, BLOCK, PAIR)
 
     with jax.named_scope("weight_grad"):
-        halves = att.reshape(N_SEQ, TOK, 2, HDIM)
-        own = jnp.where(core == 0, halves[:, :, 0], halves[:, :, 1])
-        given = jnp.where(core == 0, halves[:, :, 1], halves[:, :, 0])
-        other = lax.ppermute(given, "core", swap)
+        other = lax.ppermute(att, "core", swap)
         other_sum = lax.ppermute(grad_sum, "core", swap)
         term = call(
             term_kernel,
             "weight_term",
-            jax.ShapeDtypeStruct((N_Z, HDIM, D), BF16),
-            [vmem()] * 4,
-            vmem(),
+            jax.ShapeDtypeStruct((N_Z, N_SEQ, HDIM, PAIR), BF16),
+            [smem()] + [vmem()] * 4,
+            anywhere(),
+            [
+                pltpu.VMEM((N_Z, N_SEQ, HDIM, PAIR), BF16),
+                pltpu.SemaphoreType.DMA((N_Z,)),
+            ],
             flops=1_000_000_000,
             moved=6_000_000,
-        )(own, other, grad_sum, other_sum)
-        shard = lax.psum_scatter(
-            term.reshape(N_Z * HDIM, D), "z", scatter_dimension=0, tiled=True
-        )
+        )(core.reshape(1).astype(jnp.int32), att, other, grad_sum, other_sum)
+        shard = lax.psum_scatter(term, "z", scatter_dimension=0, tiled=True)[0]
 
     with jax.named_scope("passed"):
-        passed = lax.ppermute(grad_sum, "section", swap)
+        later = call(
+            touch_kernel,
+            "later",
+            jax.ShapeDtypeStruct((TOK, D), BF16),
+            [anywhere(), anywhere()],
+            anywhere(),
+            [pltpu.SemaphoreType.DMA(())],
+            flops=1_000_000,
+            moved=1_000_000,
+        )(grad_sum, grad_got)
+        passed = lax.ppermute(later, "section", swap)
 
     with jax.named_scope("backward"):
         grads = call(
@@ -304,16 +338,23 @@
     with jax.named_scope("grads_to_tokens"):
         back = exchange(grads.reshape(N_SEQ, 3, TOK, PAIR))
 
+    with jax.named_scope("unpack"):
+        grad_query, grad_pairs = call(
+            unpack_kernel,
+            "unpack",
+            (
+                jax.ShapeDtypeStruct((TOK, D), BF16),
+                jax.ShapeDtypeStruct((2, TOK, D), BF16),
+            ),
+            [anywhere()],
+            (anywhere(), anywhere()),
+            [pltpu.SemaphoreType.DMA((N_SEQ, 2))],
+            flops=1_000_000,
+            moved=3_000_000,
+        )(back)
+
     with jax.named_scope("weight_grad"):
-        pieces = call(
-            split_kernel,
-            "weight_split",
-            jax.ShapeDtypeStruct((N_SEQ, HDIM, PAIR), BF16),
-            [vmem(), anywhere()],
-            vmem(),
-            flops=1_000_000,
-            moved=1_000_000,
-        )(shard, back)
+        shard, grad_query = lax.optimization_barrier((shard, grad_query))
         spread = call(
             spread_kernel,
             "weight_sum",
@@ -322,7 +363,8 @@
             vmem(),
             flops=1_000_000,
             moved=1_000_000,
-        )(exchange(pieces))
+        )(exchange(shard))
+        spread, passed = lax.optimization_barrier((spread, passed))
         weight_grad = call(
             average_kernel,
             "average",
@@ -333,9 +375,12 @@
             moved=1_500_000,
         )(exchange(spread))
 
-    with jax.named_scope("unpack"):
-        back = back.transpose(1, 2, 0, 3).reshape(3, TOK, D)
-    return (back[None, :1].reshape(1, 1, TOK, D), back[None, None, 1:], passed[None, None], weight_grad[None])
+    return (
+        grad_query[None, None],
+        grad_pairs[None, None],
+        passed[None, None],
+        weight_grad[None],
+    )
 
 
 def solution(mesh):

time: 186 us -> 172 us (0.925)
  local copies, waits for them, and re-layouts: 16.8 us -> 4.93 us
  starting transfers between devices: 23.9 us -> 16.9 us
  blocking collectives: 38.3 us -> 42.4 us
    ppermute x2, waiting for transfers between devices: 12.2 us -> 0.01 us  [the longest x1 0.01 us: on_device(): other = lax.ppermute(att, 'core', swap)]
    all_to_all x4 -> x3, waiting for transfers between devices: 36.7 us -> 46.5 us  [exchange(): return lax.all_to_all(chunks, 'seq', 0, 0, tiled=True)]
    unnamed x36 -> x22, local copies, waits for them, and re-layouts: 12.4 us -> 4.52 us
    all_to_all x4 -> x3, starting transfers between devices: 21.2 us -> 14.4 us  [exchange(): return lax.all_to_all(chunks, 'seq', 0, 0, tiled=True)]
    all_to_all x2 -> x3, blocking collectives: 38.3 us -> 42.4 us  [exchange(): return lax.all_to_all(chunks, 'seq', 0, 0, tiled=True)]
    all_gather x1, waiting for transfers between devices: 4.88 us -> 7.84 us  [on_device(): w_full = lax.all_gather(w_out[0], ('z', 'core'), axis=0, tiled=True)]
    slice x5 -> x0, local copies, waits for them, and re-layouts: 2.92 us -> none  [the longest x2 2.14 us: on_device(): back[None, :1].reshape(1, 1, TOK, D)]
    pallas_call x2 -> x3, Pallas kernels: 4.23 us -> 4.54 us  [the longest x1 3.23 us: on_device(): call(term_kernel, 'weight_term', jax.ShapeDtypeStruct((N_Z, N_SEQ, HDIM,...]
  transfers between devices with their start and end apart: 9 -> 8, of which waited for: 7 -> 6; matrix products, arithmetic and copies ran while one was open for 5% -> 2% of each run, Pallas kernels for 11% -> 16%
where the time goes in v2:
time: 172 us; the launch traced here: 171 us
  waiting for transfers between devices  58.8 us (34%)
  blocking collectives  42.4 us (25%)
  Pallas kernels  32.5 us (19%)
  starting transfers between devices  16.9 us (10%)
  between operations  14.2 us (8%)
  local copies, waits for them, and re-layouts  4.93 us (3%)
    all_to_all x3, waiting for transfers between devices, exchange(): return lax.all_to_all(chunks, 'seq', 0, 0, tiled=True)  46.5 us
    all_to_all x3, blocking collectives, exchange(): return lax.all_to_all(chunks, 'seq', 0, 0, tiled=True)  42.4 us
    all_to_all x3, starting transfers between devices, exchange(): return lax.all_to_all(chunks, 'seq', 0, 0, tiled=True)  14.4 us
    pallas_call x1, Pallas kernels, on_device(): call(functools.partial(backward_kernel, 8), 'attention_backward', jax.Sha...  10.8 us
    pallas_call x1, Pallas kernels, on_device(): call(functools.partial(forward_kernel, 8), 'attention_forward', jax.Shape...  8.46 us
    all_gather x1, waiting for transfers between devices, on_device(): w_full = lax.all_gather(w_out[0], ('z', 'core'), axis=0, tiled=True)  7.84 us
    pallas_call x1, Pallas kernels, on_device(): call(project_kernel, 'project', (jax.ShapeDtypeStruct((TOK, D), BF16), ja...  6.78 us
    unnamed x22, local copies, waits for them, and re-layouts  4.52 us
  transfers between devices with their start and end apart: 8, of which 6 were waited for; matrix products, arithmetic and copies ran while one was open for 2% of the time, Pallas kernels for 16%

profile of v2, /device:TPU:8, one launch (start us, length us, event | category | flops | bytes accessed | tf_op | source)
XLA Modules:
  0.0 171.0 jit_solution(5760928606726900493)
XLA Ops:
  7.9 1.5 copy.19
  9.7 0.8 copy-done.7
  10.7 1.3 maximum_bitcast_fusion
  12.0 5.9 %all-to-all-start = ((bf16[8,3,128,256]{3,2,1,0:T(8,128)(2,1)}), bf16[8,3,128,256]{3,2,1,0:T(8,128)(2,1)S(1)}, u32[]{:S(2)}, u32[]{:S(2)}) async-start(bf16[8,3,128,256]{3,2,1,0:T(8,128)(2,1)} %maximum_bitcast_fusion), calls=%async_computation | async-start | bytes 3145728 | tf_op jit(solution)/shard_map/to_heads/all_to_all | solution.py:238
  18.1 21.5 %all-to-all-done = bf16[8,3,128,256]{3,2,1,0:T(8,128)(2,1)S(1)} async-done(((bf16[8,3,128,256]{3,2,1,0:T(8,128)(2,1)}), bf16[8,3,128,256]{3,2,1,0:T(8,128)(2,1)S(1)}, u32[]{:S(2)}, u32[]{:S(2)}) %all-to-all-start) | async-done | bytes 1572896 | tf_op jit(solution)/shard_map/to_heads/all_to_all | solution.py:238
  39.6 8.5 %attention_forward.1 = bf16[8,2,64,256]{3,2,1,0:T(8,128)(2,1)S(1)} custom-call(s32[2]{0:T(128)S(1)} %bitcast.34, s32[48]{0:T(128)S(1)} %reshape_squeeze.3.rand_ref, bf16[8,3,2,64,256]{4,3,2,1,0:T(8,128)(2,1)S(1)} %bitcast.28), custom_call_target="tpu_custom_call" | custom-call | flops 1000000000 | bytes 2000000 | tf_op jit(solution)/shard_map/forward/attention_forward/pallas_call | solution.py:256
  48.1 12.7 %all_to_all.30.att_ref.own_ref = bf16[8,128,256]{2,1,0:T(8,128)(2,1)S(1)} all-to-all(bf16[8,128,256]{2,1,0:T(8,128)(2,1)S(1)} %bitcast.33), channel_id=1, replica_groups=mesh['z'=8,'core'=2,'seq'=8,'section'=2] {'seq'}, dimensions={0} | all-to-all | bytes 1048576 | tf_op jit(solution)/shard_map/to_tokens/all_to_all | solution.py:238
  60.8 7.8 %all-gather.3.cloned.1.call-done = bf16[1,2048,2048]{2,1,0:T(8,128)(2,1)} async-done(((bf16[1,128,2048]{2,1,0:T(8,128)(2,1)}), bf16[1,2048,2048]{2,1,0:T(8,128)(2,1)}) %all-gather.3.cloned.1.call-update) | async-done | bytes 8388624 | tf_op jit(solution)/shard_map/gather_w/all_gather | solution.py:248
  68.7 6.8 %project.1 = (bf16[128,2048]{1,0:T(8,128)(2,1)S(1)}, bf16[8,128,256]{2,1,0:T(8,128)(2,1)S(1)}) custom-call(bf16[8,128,256]{2,1,0:T(8,128)(2,1)S(1)} %all_to_all.30.att_ref.own_ref, bf16[2048,2048]{1,0:T(8,128)(2,1)} %bitcast.36, bf16[128,2048]{1,0:T(8,128)(2,1)S(1)} %bitcast.31, bf16[128,2048]{1,0:T(8,128)(2,1)S(1)} %bitcast.32, f32[1,2048]{1,0:T(1,128)S(1)} %copy-done.5), custom_call_target="tpu_custom_call" | custom-call | flops 2000000000 | bytes 10000000 | tf_op jit(solution)/shard_map/project/project/pallas_call | solution.py:270
  75.8 1.7 collective-permute-done.1.other_sum_ref
  77.4 3.2 %weight_term.1 = bf16[8,8,128,256]{3,2,1,0:T(8,128)(2,1)} custom-call(s32[1]{0:T(128)} %bitcast.core_ref, bf16[8,128,256]{2,1,0:T(8,128)(2,1)S(1)} %all_to_all.30.att_ref.own_ref, bf16[8,128,256]{2,1,0:T(8,128)(2,1)S(1)} %collective-permute-done.other_ref, bf16[128,2048]{1,0:T(8,128)(2,1)S(1)} %get-tuple-element.12.own_sum_ref.rows_hbm, ...), custom_call_target="tpu_custom_call" | custom-call | flops 1000000000 | bytes 6000000 | tf_op jit(solution)/shard_map/weight_grad/weight_term/pallas_call | solution.py:294
  80.7 15.0 %all_to_all.31 = bf16[8,128,256]{2,1,0:T(8,128)(2,1)S(1)} all-to-all(bf16[8,128,256]{2,1,0:T(8,128)(2,1)S(1)} %get-tuple-element.13), channel_id=1, replica_groups=mesh['z'=8,'core'=2,'seq'=8,'section'=2] {'seq'}, dimensions={0} | all-to-all | bytes 1048576 | tf_op jit(solution)/shard_map/grad_to_heads/all_to_all | solution.py:238
  95.7 10.8 %attention_backward.1 = bf16[8,3,2,64,256]{4,3,2,1,0:T(8,128)(2,1)S(1)} custom-call(s32[2]{0:T(128)S(1)} %bitcast.35, s32[48]{0:T(128)S(1)} %reshape_squeeze.3.rand_ref, bf16[8,3,2,64,256]{4,3,2,1,0:T(8,128)(2,1)S(1)} %bitcast.29, bf16[8,2,64,256]{3,2,1,0:T(8,128)(2,1)S(1)} %bitcast.26), custom_call_target="tpu_custom_call" | custom-call | flops 3000000000 | bytes 4000000 | tf_op jit(solution)/shard_map/backward/attention_backward/pallas_call | solution.py:323
  106.5 1.2 copy-done.2
  107.6 4.3 %all-to-all-start.3 = ((bf16[8,3,128,256]{3,2,1,0:T(8,128)(2,1)}), bf16[8,3,128,256]{3,2,1,0:T(8,128)(2,1)S(1)}, u32[]{:S(2)}, u32[]{:S(2)}) async-start(bf16[8,3,128,256]{3,2,1,0:T(8,128)(2,1)} %bitcast.30), calls=%async_computation.4 | async-start | bytes 3145728 | tf_op jit(solution)/shard_map/grads_to_tokens/all_to_all | solution.py:238
  112.0 2.2 %collective-permute-start.2 = (bf16[128,2048]{1,0:T(8,128)(2,1)S(1)}, bf16[128,2048]{1,0:T(8,128)(2,1)S(1)}, u32[]{:S(2)}, u32[]{:S(2)}) collective-permute-start(bf16[128,2048]{1,0:T(8,128)(2,1)S(1)} %later.1), channel_id=1, source_target_pairs={{0,1},{1,0},{2,3},{3,2},{4,5},{5,4},{6,7},{7,6},{8,9},{9,8},{10,11... | collective-permute-start | bytes 1572872 | tf_op jit(solution)/shard_map/passed/ppermute | solution.py:320
  114.2 17.1 %all-to-all-done.3.back_hbm = bf16[8,3,128,256]{3,2,1,0:T(8,128)(2,1)S(1)} async-done(((bf16[8,3,128,256]{3,2,1,0:T(8,128)(2,1)}), bf16[8,3,128,256]{3,2,1,0:T(8,128)(2,1)S(1)}, u32[]{:S(2)}, u32[]{:S(2)}) %all-to-all-start.3) | async-done | bytes 1572896 | tf_op jit(solution)/shard_map/grads_to_tokens/all_to_all | solution.py:238
  131.3 1.3 unpack.1
  132.6 2.1 %reduce-scatter.2.cloned.1.call-done = bf16[1,8,128,256]{3,2,1,0:T(8,128)(2,1)} async-done(((bf16[8,8,128,256]{3,2,1,0:T(8,128)(2,1)}), bf16[1,8,128,256]{3,2,1,0:T(8,128)(2,1)}) %reduce-scatter.2.cloned.1.call-update) | async-done | bytes 524304 | tf_op jit(solution)/shard_map/weight_grad/reduce_scatter | solution.py:307
  134.7 14.7 %all_to_all.32.parts_ref = bf16[8,128,256]{2,1,0:T(8,128)(2,1)S(1)} all-to-all(bf16[8,128,256]{2,1,0:T(8,128)(2,1)} %bitcast.42), channel_id=1, replica_groups=mesh['z'=8,'core'=2,'seq'=8,'section'=2] {'seq'}, dimensions={0} | all-to-all | bytes 1048576 | tf_op jit(solution)/shard_map/weight_grad/all_to_all | solution.py:238
  149.4 0.9 weight_sum.1
  150.3 4.2 %all-to-all-start.5 = ((bf16[8,128,256]{2,1,0:T(8,128)(2,1)}), bf16[8,128,256]{2,1,0:T(8,128)(2,1)S(1)}, u32[]{:S(2)}, u32[]{:S(2)}) async-start(bf16[8,128,256]{2,1,0:T(8,128)(2,1)} %weight_sum.1), calls=%async_computation.6 | async-start | bytes 1048576 | tf_op jit(solution)/shard_map/weight_grad/all_to_all | solution.py:238
  154.5 7.9 %all-to-all-done.5.pieces_ref = bf16[8,128,256]{2,1,0:T(8,128)(2,1)S(1)} async-done(((bf16[8,128,256]{2,1,0:T(8,128)(2,1)}), bf16[8,128,256]{2,1,0:T(8,128)(2,1)S(1)}, u32[]{:S(2)}, u32[]{:S(2)}) %all-to-all-start.5) | async-done | bytes 524320 | tf_op jit(solution)/shard_map/weight_grad/all_to_all | solution.py:238
  162.3 1.0 average.1
  (31 shorter events, 2.5 us)
Async XLA Ops:
  7.2 61.5 %all-gather.3.cloned.1.call-start = ((), (), s32[]{:S(2)}) async-start(), calls=%async_computation.8 | async-start | bytes 8912896 | tf_op jit(solution)/shard_map/gather_w/all_gather | solution.py:248
  9.4 1.0 copy-start.7
  12.0 5.9 %copy-start.8 = (s32[1,16,3]{1,0,2:T(1,128)S(1)}, s32[1,16,3]{1,0,2:T(1,128)}, u32[]{:S(2)}) copy-start(s32[1,16,3]{1,0,2:T(1,128)} %param.15) | copy-start | bytes 580
  12.0 27.6 %copy-start.6 = (s32[1,2]{1,0:T(1,128)S(1)}, s32[1,2]{1,0:T(1,128)}, u32[]{:S(2)}) copy-start(s32[1,2]{1,0:T(1,128)} %param.14) | copy-start | bytes 28
  12.0 27.5 %all-to-all-start = ((bf16[8,3,128,256]{3,2,1,0:T(8,128)(2,1)}), bf16[8,3,128,256]{3,2,1,0:T(8,128)(2,1)S(1)}, u32[]{:S(2)}, u32[]{:S(2)}) async-start(bf16[8,3,128,256]{3,2,1,0:T(8,128)(2,1)} %maximum_bitcast_fusion), calls=%async_computation | async-start | bytes 3145728 | tf_op jit(solution)/shard_map/to_heads/all_to_all | solution.py:238
  17.9 116.8 %reduce-scatter.2.cloned.1.call-start = ((), (), s32[]{:S(2)}) async-start(), calls=%async_computation.7 | async-start | bytes 4718592 | tf_op jit(solution)/shard_map/weight_grad/reduce_scatter | solution.py:307
  39.6 8.5 %copy-start = (bf16[8,3,128,256]{3,2,1,0:T(8,128)(2,1)}, bf16[8,3,128,256]{3,2,1,0:T(8,128)(2,1)S(1)}, u32[]{:S(2)}) copy-start(bf16[8,3,128,256]{3,2,1,0:T(8,128)(2,1)S(1)} %all-to-all-done) | copy-start | bytes 4718596
  39.6 29.1 %copy-start.3 = (bf16[1,1,128,2048]{3,2,1,0:T(8,128)(2,1)S(1)}, bf16[1,1,128,2048]{3,2,1,0:T(8,128)(2,1)}, u32[]{:S(2)}) copy-start(bf16[1,1,128,2048]{3,2,1,0:T(8,128)(2,1)} %param.10) | copy-start | bytes 1572868
  39.6 29.1 %copy-start.4 = (bf16[1,1,128,2048]{3,2,1,0:T(8,128)(2,1)S(1)}, bf16[1,1,128,2048]{3,2,1,0:T(8,128)(2,1)}, u32[]{:S(2)}) copy-start(bf16[1,1,128,2048]{3,2,1,0:T(8,128)(2,1)} %param.11) | copy-start | bytes 1572868
  39.6 29.1 %copy-start.5 = (f32[1,2048]{1,0:T(1,128)S(1)}, f32[1,2048]{1,0:T(1,128)}, u32[]{:S(2)}) copy-start(f32[1,2048]{1,0:T(1,128)} %gain_ref.1) | copy-start | bytes 24580
  60.8 15.0 %collective-permute-start = (bf16[8,128,256]{2,1,0:T(8,128)(2,1)S(1)}, bf16[8,128,256]{2,1,0:T(8,128)(2,1)S(1)}, u32[]{:S(2)}, u32[]{:S(2)}) collective-permute-start(bf16[8,128,256]{2,1,0:T(8,128)(2,1)S(1)} %all_to_all.30.att_ref.own_ref), channel_id=1, source_target_pairs={{0,16},{16,0},{1,17},{17,1},{2,18},{18,2},{3,19},{19,3},{4,20},{20... | collective-permute-start | bytes 1572872 | tf_op jit(solution)/shard_map/weight_grad/ppermute | solution.py:292
  75.4 2.0 %collective-permute-start.1 = (bf16[128,2048]{1,0:T(8,128)(2,1)S(1)}, bf16[128,2048]{1,0:T(8,128)(2,1)S(1)}, u32[]{:S(2)}, u32[]{:S(2)}) collective-permute-start(bf16[128,2048]{1,0:T(8,128)(2,1)S(1)} %get-tuple-element.12.own_sum_ref.rows_hbm), channel_id=1, source_target_pairs={{0,16},{16,0},{1,17},{17,1},{2,18},{18,2},{3,19},{19,3},{4,20},{20... | collective-permute-start | bytes 1572872 | tf_op jit(solution)/shard_map/weight_grad/ppermute | solution.py:293
  80.7 15.0 %copy-start.1 = (bf16[8,3,128,256]{3,2,1,0:T(8,128)(2,1)S(1)}, bf16[8,3,128,256]{3,2,1,0:T(8,128)(2,1)}, u32[]{:S(2)}) copy-start(bf16[8,3,128,256]{3,2,1,0:T(8,128)(2,1)} %copy-done) | copy-start | bytes 4718596
  106.5 1.2 copy-start.2
  107.6 23.7 %all-to-all-start.3 = ((bf16[8,3,128,256]{3,2,1,0:T(8,128)(2,1)}), bf16[8,3,128,256]{3,2,1,0:T(8,128)(2,1)S(1)}, u32[]{:S(2)}, u32[]{:S(2)}) async-start(bf16[8,3,128,256]{3,2,1,0:T(8,128)(2,1)} %bitcast.30), calls=%async_computation.4 | async-start | bytes 3145728 | tf_op jit(solution)/shard_map/grads_to_tokens/all_to_all | solution.py:238
  112.0 38.3 %collective-permute-start.2 = (bf16[128,2048]{1,0:T(8,128)(2,1)S(1)}, bf16[128,2048]{1,0:T(8,128)(2,1)S(1)}, u32[]{:S(2)}, u32[]{:S(2)}) collective-permute-start(bf16[128,2048]{1,0:T(8,128)(2,1)S(1)} %later.1), channel_id=1, source_target_pairs={{0,1},{1,0},{2,3},{3,2},{4,5},{5,4},{6,7},{7,6},{8,9},{9,8},{10,11... | collective-permute-start | bytes 1572872 | tf_op jit(solution)/shard_map/passed/ppermute | solution.py:320
  150.3 12.0 %all-to-all-start.5 = ((bf16[8,128,256]{2,1,0:T(8,128)(2,1)}), bf16[8,128,256]{2,1,0:T(8,128)(2,1)S(1)}, u32[]{:S(2)}, u32[]{:S(2)}) async-start(bf16[8,128,256]{2,1,0:T(8,128)(2,1)} %weight_sum.1), calls=%async_computation.6 | async-start | bytes 1048576 | tf_op jit(solution)/shard_map/weight_grad/all_to_all | solution.py:238
Sparse Core Ops, SparseCore 0:
  9.8 58.7 all-gather.2
  80.8 53.8 reduce-scatter.1

commit v3 on v2

--- a/solution.py
+++ b/solution.py
@@ -18,6 +18,7 @@
 NBLK = N_SEQ * QB
 PAIR = 2 * HDIM
 D = 2048
+STAGE = 2
 N_Z = 8
 BATCH = 16
 TOK = QB * BLOCK
@@ -134,7 +135,9 @@
     lax.fori_loop(0, NBLK, finish, 0)
 
 
-def project_kernel(att_ref, w_hbm, resid_ref, up_ref, gain_ref, sum_ref, ga_ref, w_vmem, total, sems):
+def project_kernel(
+    att_ref, w_hbm, resid_ref, up_ref, gain_ref, sum_hbm, ga_ref, w_vmem, total, held, sems, sum_sem
+):
     copies = [
         pltpu.make_async_copy(
             w_hbm.at[pl.ds(s * PAIR, PAIR)], w_vmem.at[pl.ds(s * PAIR, PAIR)], sems.at[s]
@@ -143,28 +146,34 @@
     ]
     for copy in copies:
         copy.start()
-    total[...] = resid_ref[...].astype(F32)
-    for s in range(N_SEQ):
-        copies[s].wait()
-        total[...] += dot(att_ref[s], w_vmem[s * PAIR : (s + 1) * PAIR], ((1,), (0,)))
+    for s in range(0, N_SEQ, STAGE):
+        for n in range(s, s + STAGE):
+            copies[n].wait()
+        att = jnp.concatenate([att_ref[n] for n in range(s, s + STAGE)], axis=1)
+        part = dot(att, w_vmem[s * PAIR : (s + STAGE) * PAIR], ((1,), (0,)))
+        total[...] = part + (resid_ref[...].astype(F32) if s == 0 else total[...])
     summed = total[...]
     inverse = lax.rsqrt(jnp.mean(summed * summed, axis=-1, keepdims=True) + 1e-06)
     scaled = up_ref[...].astype(F32) * gain_ref[...]
     inner = jnp.mean(scaled * summed, axis=-1, keepdims=True)
     grad_sum = (inverse * scaled - summed * (inverse * inverse * inverse * inner)).astype(BF16)
-    sum_ref[...] = grad_sum
+    held[...] = grad_sum
+    out = pltpu.make_async_copy(held, sum_hbm, sum_sem)
+    out.start()
     for s in range(N_SEQ):
         part = dot(grad_sum, w_vmem[s * PAIR : (s + 1) * PAIR], ((1,), (1,)))
         ga_ref[s] = part.astype(BF16)
-
-
-def term_kernel(core_ref, own_ref, other_ref, own_sum_ref, other_sum_ref, out_hbm, held, sems):
+    out.wait()
+
+
+def term_kernel(core_ref, own_ref, other_ref, own_sum_ref, other_sum_ref, out_hbm, held, sums, sems):
     columns = pl.ds(pl.multiple_of(core_ref[0] * HDIM, HDIM), HDIM)
+    sums[:TOK] = own_sum_ref[...]
+    sums[TOK:] = other_sum_ref[...]
     copies = []
     for n in range(N_Z):
-        part = dot(own_ref[n, :, columns], own_sum_ref[...], ((0,), (0,)))
-        part += dot(other_ref[n, :, columns], other_sum_ref[...], ((0,), (0,)))
-        part = part.astype(BF16)
+        both = jnp.concatenate([own_ref[n, :, columns], other_ref[n, :, columns]], axis=0)
+        part = dot(both, sums[...], ((0,), (0,))).astype(BF16)
         for s in range(N_SEQ):
             held[n, s] = part[:, s * PAIR : (s + 1) * PAIR]
         copies.append(pltpu.make_async_copy(held.at[n], out_hbm.at[n], sems.at[n]))
@@ -173,7 +182,8 @@
         copy.wait()
 
 
-def touch_kernel(rows_hbm, after_hbm, out_hbm, sem):
+def touch_kernel(rows_hbm, *refs):
+    out_hbm, sem = refs[-2:]
     copy = pltpu.make_async_copy(rows_hbm, out_hbm, sem)
     copy.start()
     copy.wait()
@@ -204,13 +214,23 @@
         out_ref[s] = total
 
 
-def average_kernel(pieces_ref, out_ref):
+def average_kernel(pieces_ref, out_hbm, held, sems):
+    copies = []
     for s in range(N_SEQ):
-        out_ref[:, s * PAIR : (s + 1) * PAIR] = pieces_ref[s].astype(F32) * (1.0 / BATCH)
+        at = pl.ds(s * PAIR, PAIR)
+        held[:, at] = pieces_ref[s].astype(F32) * (1.0 / BATCH)
+        copies.append(pltpu.make_async_copy(held.at[:, at], out_hbm.at[:, at], sems.at[s]))
+        copies[-1].start()
+    for copy in copies:
+        copy.wait()
 
 
 def vmem():
     return pl.BlockSpec(memory_space=pltpu.VMEM)
+
+
+def hbm():
+    return pl.BlockSpec(memory_space=pltpu.HBM)
 
 
 def anywhere():
@@ -234,6 +254,19 @@
     )
 
 
+def copied(rows, *after):
+    return call(
+        touch_kernel,
+        "copied",
+        jax.ShapeDtypeStruct(rows.shape, rows.dtype),
+        [anywhere()] * (1 + len(after)),
+        anywhere(),
+        [pltpu.SemaphoreType.DMA(())],
+        flops=1_000_000,
+        moved=1_000_000,
+    )(rows, *after)
+
+
 def exchange(chunks):
     return lax.all_to_all(chunks, "seq", 0, 0, tiled=True)
 
@@ -275,11 +308,13 @@
                 jax.ShapeDtypeStruct((N_SEQ, TOK, PAIR), BF16),
             ),
             [vmem(), anywhere(), vmem(), vmem(), vmem()],
-            (vmem(), vmem()),
+            (hbm(), vmem()),
             [
                 pltpu.VMEM((D, D), BF16),
                 pltpu.VMEM((TOK, D), F32),
+                pltpu.VMEM((TOK, D), BF16),
                 pltpu.SemaphoreType.DMA((N_SEQ,)),
+                pltpu.SemaphoreType.DMA(()),
             ],
             flops=2_000_000_000,
             moved=10_000_000,
@@ -299,6 +334,7 @@
             anywhere(),
             [
                 pltpu.VMEM((N_Z, N_SEQ, HDIM, PAIR), BF16),
+                pltpu.VMEM((2 * TOK, D), BF16),
                 pltpu.SemaphoreType.DMA((N_Z,)),
             ],
             flops=1_000_000_000,
@@ -307,17 +343,7 @@
         shard = lax.psum_scatter(term, "z", scatter_dimension=0, tiled=True)[0]
 
     with jax.named_scope("passed"):
-        later = call(
-            touch_kernel,
-            "later",
-            jax.ShapeDtypeStruct((TOK, D), BF16),
-            [anywhere(), anywhere()],
-            anywhere(),
-            [pltpu.SemaphoreType.DMA(())],
-            flops=1_000_000,
-            moved=1_000_000,
-        )(grad_sum, grad_got)
-        passed = lax.ppermute(later, "section", swap)
+        passed = lax.ppermute(copied(grad_sum, grad_got), "section", swap)
 
     with jax.named_scope("backward"):
         grads = call(
@@ -338,6 +364,7 @@
     with jax.named_scope("grads_to_tokens"):
         back = exchange(grads.reshape(N_SEQ, 3, TOK, PAIR))
 
+    shard, back = lax.optimization_barrier((shard, back))
     with jax.named_scope("unpack"):
         grad_query, grad_pairs = call(
             unpack_kernel,
@@ -354,7 +381,6 @@
         )(back)
 
     with jax.named_scope("weight_grad"):
-        shard, grad_query = lax.optimization_barrier((shard, grad_query))
         spread = call(
             spread_kernel,
             "weight_sum",
@@ -370,7 +396,8 @@
             "average",
             jax.ShapeDtypeStruct((HDIM, D), F32),
             [vmem()],
-            vmem(),
+            hbm(),
+            [pltpu.VMEM((HDIM, D), F32), pltpu.SemaphoreType.DMA((N_SEQ,))],
             flops=1_000_000,
             moved=1_500_000,
         )(exchange(spread))
@@ -378,7 +405,7 @@
     return (
         grad_query[None, None],
         grad_pairs[None, None],
-        passed[None, None],
+        copied(passed)[None, None],
         weight_grad[None],
     )
 

time: 172 us -> 170 us (0.988)
    all_to_all x3, waiting for transfers between devices: 46.5 us -> 44.4 us  [exchange(): return lax.all_to_all(chunks, 'seq', 0, 0, tiled=True)]
    unnamed x22 -> x21, local copies, waits for them, and re-layouts: 4.52 us -> 3.73 us
  transfers between devices with their start and end apart: 8 -> 8, of which waited for: 6 -> 6; matrix products, arithmetic and copies ran while one was open for 2% -> 2% of each run, Pallas kernels for 16% -> 17%
where the time goes in v3:
time: 170 us
  waiting for transfers between devices  58 us (34%)
  blocking collectives  42.4 us (25%)
  Pallas kernels  32.7 us (19%)
  starting transfers between devices  17 us (10%)
  between operations  14.2 us (8%)
  local copies, waits for them, and re-layouts  4.14 us (2%)
    all_to_all x3, waiting for transfers between devices, exchange(): return lax.all_to_all(chunks, 'seq', 0, 0, tiled=True)  44.4 us
    all_to_all x3, blocking collectives, exchange(): return lax.all_to_all(chunks, 'seq', 0, 0, tiled=True)  42.4 us
    all_to_all x3, starting transfers between devices, exchange(): return lax.all_to_all(chunks, 'seq', 0, 0, tiled=True)  14.4 us
    pallas_call x1, Pallas kernels, on_device(): call(functools.partial(backward_kernel, 8), 'attention_backward', jax.Sha...  10.8 us
    pallas_call x1, Pallas kernels, on_device(): call(functools.partial(forward_kernel, 8), 'attention_forward', jax.Shape...  8.46 us
    all_gather x1, waiting for transfers between devices, on_device(): w_full = lax.all_gather(w_out[0], ('z', 'core'), axis=0, tiled=True)  7.84 us
    pallas_call x1, Pallas kernels, on_device(): call(project_kernel, 'project', (jax.ShapeDtypeStruct((TOK, D), BF16), ja...  7.1 us
    unnamed x21, local copies, waits for them, and re-layouts  3.73 us
  transfers between devices with their start and end apart: 8, of which 6 were waited for; matrix products, arithmetic and copies ran while one was open for 2% of the time, Pallas kernels for 17%

profile of v3, /device:TPU:8, one launch (start us, length us, event | category | flops | bytes accessed | tf_op | source)
XLA Modules:
  0.0 169.7 jit_solution(12576679398894779188)
XLA Ops:
  7.9 1.5 copy.19
  10.7 1.3 maximum_bitcast_fusion
  12.0 5.9 %all-to-all-start = ((bf16[8,3,128,256]{3,2,1,0:T(8,128)(2,1)}), bf16[8,3,128,256]{3,2,1,0:T(8,128)(2,1)S(1)}, u32[]{:S(2)}, u32[]{:S(2)}) async-start(bf16[8,3,128,256]{3,2,1,0:T(8,128)(2,1)} %maximum_bitcast_fusion), calls=%async_computation | async-start | bytes 3145728 | tf_op jit(solution)/shard_map/to_heads/all_to_all | solution.py:271
  18.1 21.5 %all-to-all-done = bf16[8,3,128,256]{3,2,1,0:T(8,128)(2,1)S(1)} async-done(((bf16[8,3,128,256]{3,2,1,0:T(8,128)(2,1)}), bf16[8,3,128,256]{3,2,1,0:T(8,128)(2,1)S(1)}, u32[]{:S(2)}, u32[]{:S(2)}) %all-to-all-start) | async-done | bytes 1572896 | tf_op jit(solution)/shard_map/to_heads/all_to_all | solution.py:271
  39.6 8.5 %attention_forward.1 = bf16[8,2,64,256]{3,2,1,0:T(8,128)(2,1)S(1)} custom-call(s32[2]{0:T(128)S(1)} %bitcast.34, s32[48]{0:T(128)S(1)} %reshape_squeeze.3.rand_ref, bf16[8,3,2,64,256]{4,3,2,1,0:T(8,128)(2,1)S(1)} %bitcast.28), custom_call_target="tpu_custom_call" | custom-call | flops 1000000000 | bytes 2000000 | tf_op jit(solution)/shard_map/forward/attention_forward/pallas_call | solution.py:289
  48.1 12.7 %all_to_all.30.att_ref.own_ref = bf16[8,128,256]{2,1,0:T(8,128)(2,1)S(1)} all-to-all(bf16[8,128,256]{2,1,0:T(8,128)(2,1)S(1)} %bitcast.33), channel_id=1, replica_groups=mesh['z'=8,'core'=2,'seq'=8,'section'=2] {'seq'}, dimensions={0} | all-to-all | bytes 1048576 | tf_op jit(solution)/shard_map/to_tokens/all_to_all | solution.py:271
  60.8 7.8 %all-gather.3.cloned.1.call-done = bf16[1,2048,2048]{2,1,0:T(8,128)(2,1)} async-done(((bf16[1,128,2048]{2,1,0:T(8,128)(2,1)}), bf16[1,2048,2048]{2,1,0:T(8,128)(2,1)}) %all-gather.3.cloned.1.call-update) | async-done | bytes 8388624 | tf_op jit(solution)/shard_map/gather_w/all_gather | solution.py:281
  68.7 7.1 %project.1 = (bf16[128,2048]{1,0:T(8,128)(2,1)S(1)}, bf16[8,128,256]{2,1,0:T(8,128)(2,1)S(1)}) custom-call(bf16[8,128,256]{2,1,0:T(8,128)(2,1)S(1)} %all_to_all.30.att_ref.own_ref, bf16[2048,2048]{1,0:T(8,128)(2,1)} %bitcast.36, bf16[128,2048]{1,0:T(8,128)(2,1)S(1)} %bitcast.31, bf16[128,2048]{1,0:T(8,128)(2,1)S(1)} %bitcast.32, f32[1,2048]{1,0:T(1,128)S(1)} %copy-done.5), custom_call_target="tpu_custom_call" | custom-call | flops 2000000000 | bytes 10000000 | tf_op jit(solution)/shard_map/project/project/pallas_call | solution.py:303
  76.1 1.6 collective-permute-done.1.other_sum_ref
  77.8 2.3 %weight_term.1 = bf16[8,8,128,256]{3,2,1,0:T(8,128)(2,1)} custom-call(s32[1]{0:T(128)} %bitcast.core_ref, bf16[8,128,256]{2,1,0:T(8,128)(2,1)S(1)} %all_to_all.30.att_ref.own_ref, bf16[8,128,256]{2,1,0:T(8,128)(2,1)S(1)} %collective-permute-done.other_ref, bf16[128,2048]{1,0:T(8,128)(2,1)S(1)} %get-tuple-element.12.own_sum_ref.rows_hbm, ...), custom_call_target="tpu_custom_call" | custom-call | flops 1000000000 | bytes 6000000 | tf_op jit(solution)/shard_map/weight_grad/weight_term/pallas_call | solution.py:329
  80.2 15.0 %all_to_all.31 = bf16[8,128,256]{2,1,0:T(8,128)(2,1)S(1)} all-to-all(bf16[8,128,256]{2,1,0:T(8,128)(2,1)S(1)} %get-tuple-element.13), channel_id=1, replica_groups=mesh['z'=8,'core'=2,'seq'=8,'section'=2] {'seq'}, dimensions={0} | all-to-all | bytes 1048576 | tf_op jit(solution)/shard_map/grad_to_heads/all_to_all | solution.py:271
  95.1 10.8 %attention_backward.1 = bf16[8,3,2,64,256]{4,3,2,1,0:T(8,128)(2,1)S(1)} custom-call(s32[2]{0:T(128)S(1)} %bitcast.35, s32[48]{0:T(128)S(1)} %reshape_squeeze.3.rand_ref, bf16[8,3,2,64,256]{4,3,2,1,0:T(8,128)(2,1)S(1)} %bitcast.29, bf16[8,2,64,256]{3,2,1,0:T(8,128)(2,1)S(1)} %bitcast.26), custom_call_target="tpu_custom_call" | custom-call | flops 3000000000 | bytes 4000000 | tf_op jit(solution)/shard_map/backward/attention_backward/pallas_call | solution.py:349
  105.9 1.2 copy-done.2
  107.1 4.3 %all-to-all-start.3 = ((bf16[8,3,128,256]{3,2,1,0:T(8,128)(2,1)}), bf16[8,3,128,256]{3,2,1,0:T(8,128)(2,1)S(1)}, u32[]{:S(2)}, u32[]{:S(2)}) async-start(bf16[8,3,128,256]{3,2,1,0:T(8,128)(2,1)} %bitcast.30), calls=%async_computation.4 | async-start | bytes 3145728 | tf_op jit(solution)/shard_map/grads_to_tokens/all_to_all | solution.py:271
  111.4 2.2 %collective-permute-start.2 = (bf16[128,2048]{1,0:T(8,128)(2,1)S(1)}, bf16[128,2048]{1,0:T(8,128)(2,1)S(1)}, u32[]{:S(2)}, u32[]{:S(2)}) collective-permute-start(bf16[128,2048]{1,0:T(8,128)(2,1)S(1)} %copied.2), channel_id=1, source_target_pairs={{0,1},{1,0},{2,3},{3,2},{4,5},{5,4},{6,7},{7,6},{8,9},{9,8},{10,11... | collective-permute-start | bytes 1572872 | tf_op jit(solution)/shard_map/passed/ppermute | solution.py:346
  113.7 17.1 %all-to-all-done.3.back_hbm = bf16[8,3,128,256]{3,2,1,0:T(8,128)(2,1)S(1)} async-done(((bf16[8,3,128,256]{3,2,1,0:T(8,128)(2,1)}), bf16[8,3,128,256]{3,2,1,0:T(8,128)(2,1)S(1)}, u32[]{:S(2)}, u32[]{:S(2)}) %all-to-all-start.3) | async-done | bytes 1572896 | tf_op jit(solution)/shard_map/grads_to_tokens/all_to_all | solution.py:271
  130.8 3.4 %reduce-scatter.2.cloned.1.call-done = bf16[1,8,128,256]{3,2,1,0:T(8,128)(2,1)} async-done(((bf16[8,8,128,256]{3,2,1,0:T(8,128)(2,1)}), bf16[1,8,128,256]{3,2,1,0:T(8,128)(2,1)}) %reduce-scatter.2.cloned.1.call-update) | async-done | bytes 524304 | tf_op jit(solution)/shard_map/weight_grad/reduce_scatter | solution.py:343
  134.2 14.7 %all_to_all.32.parts_ref = bf16[8,128,256]{2,1,0:T(8,128)(2,1)S(1)} all-to-all(bf16[8,128,256]{2,1,0:T(8,128)(2,1)} %bitcast.42), channel_id=1, replica_groups=mesh['z'=8,'core'=2,'seq'=8,'section'=2] {'seq'}, dimensions={0} | all-to-all | bytes 1048576 | tf_op jit(solution)/shard_map/weight_grad/all_to_all | solution.py:271
  148.9 0.9 weight_sum.1
  149.8 4.2 %all-to-all-start.5 = ((bf16[8,128,256]{2,1,0:T(8,128)(2,1)}), bf16[8,128,256]{2,1,0:T(8,128)(2,1)S(1)}, u32[]{:S(2)}, u32[]{:S(2)}) async-start(bf16[8,128,256]{2,1,0:T(8,128)(2,1)} %weight_sum.1), calls=%async_computation.6 | async-start | bytes 1048576 | tf_op jit(solution)/shard_map/weight_grad/all_to_all | solution.py:271
  153.9 1.3 unpack.1
  155.2 0.8 copied.3
  156.0 5.8 %all-to-all-done.5.pieces_ref = bf16[8,128,256]{2,1,0:T(8,128)(2,1)S(1)} async-done(((bf16[8,128,256]{2,1,0:T(8,128)(2,1)}), bf16[8,128,256]{2,1,0:T(8,128)(2,1)S(1)}, u32[]{:S(2)}, u32[]{:S(2)}) %all-to-all-start.5) | async-done | bytes 524320 | tf_op jit(solution)/shard_map/weight_grad/all_to_all | solution.py:271
  161.8 1.0 average.1
  (31 shorter events, 2.6 us)
Async XLA Ops:
  7.2 61.5 %all-gather.3.cloned.1.call-start = ((), (), s32[]{:S(2)}) async-start(), calls=%async_computation.8 | async-start | bytes 8912896 | tf_op jit(solution)/shard_map/gather_w/all_gather | solution.py:281
  9.4 1.0 copy-start.7
  12.0 5.9 %copy-start.8 = (s32[1,16,3]{1,0,2:T(1,128)S(1)}, s32[1,16,3]{1,0,2:T(1,128)}, u32[]{:S(2)}) copy-start(s32[1,16,3]{1,0,2:T(1,128)} %param.15) | copy-start | bytes 580
  12.0 27.6 %copy-start.6 = (s32[1,2]{1,0:T(1,128)S(1)}, s32[1,2]{1,0:T(1,128)}, u32[]{:S(2)}) copy-start(s32[1,2]{1,0:T(1,128)} %param.14) | copy-start | bytes 28
  12.0 27.5 %all-to-all-start = ((bf16[8,3,128,256]{3,2,1,0:T(8,128)(2,1)}), bf16[8,3,128,256]{3,2,1,0:T(8,128)(2,1)S(1)}, u32[]{:S(2)}, u32[]{:S(2)}) async-start(bf16[8,3,128,256]{3,2,1,0:T(8,128)(2,1)} %maximum_bitcast_fusion), calls=%async_computation | async-start | bytes 3145728 | tf_op jit(solution)/shard_map/to_heads/all_to_all | solution.py:271
  17.9 116.2 %reduce-scatter.2.cloned.1.call-start = ((), (), s32[]{:S(2)}) async-start(), calls=%async_computation.7 | async-start | bytes 4718592 | tf_op jit(solution)/shard_map/weight_grad/reduce_scatter | solution.py:343
  39.6 8.5 %copy-start = (bf16[8,3,128,256]{3,2,1,0:T(8,128)(2,1)}, bf16[8,3,128,256]{3,2,1,0:T(8,128)(2,1)S(1)}, u32[]{:S(2)}) copy-start(bf16[8,3,128,256]{3,2,1,0:T(8,128)(2,1)S(1)} %all-to-all-done) | copy-start | bytes 4718596
  39.6 29.1 %copy-start.3 = (bf16[1,1,128,2048]{3,2,1,0:T(8,128)(2,1)S(1)}, bf16[1,1,128,2048]{3,2,1,0:T(8,128)(2,1)}, u32[]{:S(2)}) copy-start(bf16[1,1,128,2048]{3,2,1,0:T(8,128)(2,1)} %param.10) | copy-start | bytes 1572868
  39.6 29.1 %copy-start.4 = (bf16[1,1,128,2048]{3,2,1,0:T(8,128)(2,1)S(1)}, bf16[1,1,128,2048]{3,2,1,0:T(8,128)(2,1)}, u32[]{:S(2)}) copy-start(bf16[1,1,128,2048]{3,2,1,0:T(8,128)(2,1)} %param.11) | copy-start | bytes 1572868
  39.6 29.1 %copy-start.5 = (f32[1,2048]{1,0:T(1,128)S(1)}, f32[1,2048]{1,0:T(1,128)}, u32[]{:S(2)}) copy-start(f32[1,2048]{1,0:T(1,128)} %gain_ref.1) | copy-start | bytes 24580
  60.8 15.3 %collective-permute-start = (bf16[8,128,256]{2,1,0:T(8,128)(2,1)S(1)}, bf16[8,128,256]{2,1,0:T(8,128)(2,1)S(1)}, u32[]{:S(2)}, u32[]{:S(2)}) collective-permute-start(bf16[8,128,256]{2,1,0:T(8,128)(2,1)S(1)} %all_to_all.30.att_ref.own_ref), channel_id=1, source_target_pairs={{0,16},{16,0},{1,17},{17,1},{2,18},{18,2},{3,19},{19,3},{4,20},{20... | collective-permute-start | bytes 1572872 | tf_op jit(solution)/shard_map/weight_grad/ppermute | solution.py:327
  75.8 2.0 %collective-permute-start.1 = (bf16[128,2048]{1,0:T(8,128)(2,1)S(1)}, bf16[128,2048]{1,0:T(8,128)(2,1)S(1)}, u32[]{:S(2)}, u32[]{:S(2)}) collective-permute-start(bf16[128,2048]{1,0:T(8,128)(2,1)S(1)} %get-tuple-element.12.own_sum_ref.rows_hbm), channel_id=1, source_target_pairs={{0,16},{16,0},{1,17},{17,1},{2,18},{18,2},{3,19},{19,3},{4,20},{20... | collective-permute-start | bytes 1572872 | tf_op jit(solution)/shard_map/weight_grad/ppermute | solution.py:328
  80.1 15.0 %copy-start.1 = (bf16[8,3,128,256]{3,2,1,0:T(8,128)(2,1)S(1)}, bf16[8,3,128,256]{3,2,1,0:T(8,128)(2,1)}, u32[]{:S(2)}) copy-start(bf16[8,3,128,256]{3,2,1,0:T(8,128)(2,1)} %copy-done) | copy-start | bytes 4718596
  105.9 1.2 copy-start.2
  107.1 23.7 %all-to-all-start.3 = ((bf16[8,3,128,256]{3,2,1,0:T(8,128)(2,1)}), bf16[8,3,128,256]{3,2,1,0:T(8,128)(2,1)S(1)}, u32[]{:S(2)}, u32[]{:S(2)}) async-start(bf16[8,3,128,256]{3,2,1,0:T(8,128)(2,1)} %bitcast.30), calls=%async_computation.4 | async-start | bytes 3145728 | tf_op jit(solution)/shard_map/grads_to_tokens/all_to_all | solution.py:271
  111.4 38.3 %collective-permute-start.2 = (bf16[128,2048]{1,0:T(8,128)(2,1)S(1)}, bf16[128,2048]{1,0:T(8,128)(2,1)S(1)}, u32[]{:S(2)}, u32[]{:S(2)}) collective-permute-start(bf16[128,2048]{1,0:T(8,128)(2,1)S(1)} %copied.2), channel_id=1, source_target_pairs={{0,1},{1,0},{2,3},{3,2},{4,5},{5,4},{6,7},{7,6},{8,9},{9,8},{10,11... | collective-permute-start | bytes 1572872 | tf_op jit(solution)/shard_map/passed/ppermute | solution.py:346
  149.8 12.0 %all-to-all-start.5 = ((bf16[8,128,256]{2,1,0:T(8,128)(2,1)}), bf16[8,128,256]{2,1,0:T(8,128)(2,1)S(1)}, u32[]{:S(2)}, u32[]{:S(2)}) async-start(bf16[8,128,256]{2,1,0:T(8,128)(2,1)} %weight_sum.1), calls=%async_computation.6 | async-start | bytes 1048576 | tf_op jit(solution)/shard_map/weight_grad/all_to_all | solution.py:271
Sparse Core Ops, SparseCore 0:
  9.8 58.7 all-gather.2
  80.3 53.8 reduce-scatter.1

commit v4 on v3

--- a/solution.py
+++ b/solution.py
@@ -135,35 +135,38 @@
     lax.fori_loop(0, NBLK, finish, 0)
 
 
-def project_kernel(
-    att_ref, w_hbm, resid_ref, up_ref, gain_ref, sum_hbm, ga_ref, w_vmem, total, held, sems, sum_sem
-):
-    copies = [
-        pltpu.make_async_copy(
-            w_hbm.at[pl.ds(s * PAIR, PAIR)], w_vmem.at[pl.ds(s * PAIR, PAIR)], sems.at[s]
-        )
-        for s in range(N_SEQ)
-    ]
+def weight_copies(w_hbm, w_vmem, sems):
+    copies = []
+    for n in range(N_SEQ // STAGE):
+        rows = pl.ds(n * STAGE * PAIR, STAGE * PAIR)
+        copies.append(pltpu.make_async_copy(w_hbm.at[rows], w_vmem.at[rows], sems.at[n]))
     for copy in copies:
         copy.start()
-    for s in range(0, N_SEQ, STAGE):
-        for n in range(s, s + STAGE):
-            copies[n].wait()
-        att = jnp.concatenate([att_ref[n] for n in range(s, s + STAGE)], axis=1)
-        part = dot(att, w_vmem[s * PAIR : (s + STAGE) * PAIR], ((1,), (0,)))
-        total[...] = part + (resid_ref[...].astype(F32) if s == 0 else total[...])
+    return copies
+
+
+def project_kernel(att_ref, w_hbm, resid_ref, up_ref, gain_ref, sum_ref, w_vmem, total, sems):
+    copies = weight_copies(w_hbm, w_vmem, sems)
+    for n in range(N_SEQ // STAGE):
+        copies[n].wait()
+        att = jnp.concatenate([att_ref[s] for s in range(n * STAGE, (n + 1) * STAGE)], axis=1)
+        part = dot(att, w_vmem[n * STAGE * PAIR : (n + 1) * STAGE * PAIR], ((1,), (0,)))
+        total[...] = part + (resid_ref[...].astype(F32) if n == 0 else total[...])
     summed = total[...]
     inverse = lax.rsqrt(jnp.mean(summed * summed, axis=-1, keepdims=True) + 1e-06)
     scaled = up_ref[...].astype(F32) * gain_ref[...]
     inner = jnp.mean(scaled * summed, axis=-1, keepdims=True)
-    grad_sum = (inverse * scaled - summed * (inverse * inverse * inverse * inner)).astype(BF16)
-    held[...] = grad_sum
-    out = pltpu.make_async_copy(held, sum_hbm, sum_sem)
-    out.start()
-    for s in range(N_SEQ):
-        part = dot(grad_sum, w_vmem[s * PAIR : (s + 1) * PAIR], ((1,), (1,)))
-        ga_ref[s] = part.astype(BF16)
-    out.wait()
+    grad_sum = inverse * scaled - summed * (inverse * inverse * inverse * inner)
+    sum_ref[...] = grad_sum.astype(BF16)
+
+
+def grad_kernel(sum_ref, w_hbm, ga_ref, w_vmem, sems):
+    copies = weight_copies(w_hbm, w_vmem, sems)
+    for n in range(N_SEQ // STAGE):
+        copies[n].wait()
+        for s in range(n * STAGE, (n + 1) * STAGE):
+            part = dot(sum_ref[...], w_vmem[s * PAIR : (s + 1) * PAIR], ((1,), (1,)))
+            ga_ref[s] = part.astype(BF16)
 
 
 def term_kernel(core_ref, own_ref, other_ref, own_sum_ref, other_sum_ref, out_hbm, held, sums, sems):
@@ -300,25 +303,27 @@
         att = exchange(att.reshape(N_SEQ, TOK, PAIR))
 
     with jax.named_scope("project"):
-        grad_sum, grad_att = call(
+        scratch = [pltpu.VMEM((D, D), BF16), pltpu.SemaphoreType.DMA((N_SEQ // STAGE,))]
+        grad_sum = call(
             project_kernel,
             "project",
-            (
-                jax.ShapeDtypeStruct((TOK, D), BF16),
-                jax.ShapeDtypeStruct((N_SEQ, TOK, PAIR), BF16),
-            ),
+            jax.ShapeDtypeStruct((TOK, D), BF16),
             [vmem(), anywhere(), vmem(), vmem(), vmem()],
-            (hbm(), vmem()),
-            [
-                pltpu.VMEM((D, D), BF16),
-                pltpu.VMEM((TOK, D), F32),
-                pltpu.VMEM((TOK, D), BF16),
-                pltpu.SemaphoreType.DMA((N_SEQ,)),
-                pltpu.SemaphoreType.DMA(()),
-            ],
-            flops=2_000_000_000,
-            moved=10_000_000,
+            vmem(),
+            [scratch[0], pltpu.VMEM((TOK, D), F32), scratch[1]],
+            flops=1_000_000_000,
+            moved=9_000_000,
         )(att, w_full, resid[0, 0], upstream[0, 0], gain)
+        grad_att = call(
+            grad_kernel,
+            "grad_attended",
+            jax.ShapeDtypeStruct((N_SEQ, TOK, PAIR), BF16),
+            [vmem(), anywhere()],
+            vmem(),
+            scratch,
+            flops=1_000_000_000,
+            moved=9_000_000,
+        )(grad_sum, w_full)
 
     with jax.named_scope("grad_to_heads"):
         grad_got = exchange(grad_att).reshape(N_SEQ, QB, BLOCK, PAIR)
@@ -343,7 +348,7 @@
         shard = lax.psum_scatter(term, "z", scatter_dimension=0, tiled=True)[0]
 
     with jax.named_scope("passed"):
-        passed = lax.ppermute(copied(grad_sum, grad_got), "section", swap)
+        passed = lax.ppermute(grad_sum, "section", swap)
 
     with jax.named_scope("backward"):
         grads = call(
@@ -361,6 +366,7 @@
             moved=4_000_000,
         )(glob_ids, rand_ids, got, grad_got)
 
+    grads, passed = lax.optimization_barrier((grads, passed))
     with jax.named_scope("grads_to_tokens"):
         back = exchange(grads.reshape(N_SEQ, 3, TOK, PAIR))
 
@@ -390,7 +396,6 @@
             flops=1_000_000,
             moved=1_000_000,
         )(exchange(shard))
-        spread, passed = lax.optimization_barrier((spread, passed))
         weight_grad = call(
             average_kernel,
             "average",

time: 170 us -> 170 us (level)
  waiting for transfers between devices: 58 us -> 45.3 us
  blocking collectives: 42.4 us -> 50.3 us
  Pallas kernels: 32.7 us -> 36.8 us
    all_to_all x3, waiting for transfers between devices: 44.4 us -> 34.2 us  [exchange(): return lax.all_to_all(chunks, 'seq', 0, 0, tiled=True)]
    all_to_all x3, blocking collectives: 42.4 us -> 50.3 us  [exchange(): return lax.all_to_all(chunks, 'seq', 0, 0, tiled=True)]
    reduce_scatter x1, waiting for transfers between devices: 3.37 us -> 0.01 us  [on_device(): shard = lax.psum_scatter(term, 'z', scatter_dimension=0, tiled=True)[0]]
    pallas_call x1 -> x2, Pallas kernels: 7.1 us -> 10.1 us  [the longest x1 5.81 us: on_device(): call(grad_kernel, 'grad_attended', jax.ShapeDtypeStruct((N_SEQ, TOK, PAIR...]
    unnamed x21 -> x15, local copies, waits for them, and re-layouts: 3.73 us -> 2.6 us
  transfers between devices with their start and end apart: 8 -> 8, of which waited for: 6 -> 5; matrix products, arithmetic and copies ran while one was open for 2% -> 2% of each run, Pallas kernels for 17% -> 19%
where the time goes in v4:
time: 170 us; the launch traced here: 169 us
  blocking collectives  50.3 us (30%)
  waiting for transfers between devices  45.3 us (27%)
  Pallas kernels  36.8 us (22%)
  starting transfers between devices  18.3 us (11%)
  between operations  14.2 us (8%)
  local copies, waits for them, and re-layouts  3.01 us (2%)
    all_to_all x3, blocking collectives, exchange(): return lax.all_to_all(chunks, 'seq', 0, 0, tiled=True)  50.3 us
    all_to_all x3, waiting for transfers between devices, exchange(): return lax.all_to_all(chunks, 'seq', 0, 0, tiled=True)  34.2 us
    all_to_all x3, starting transfers between devices, exchange(): return lax.all_to_all(chunks, 'seq', 0, 0, tiled=True)  15.8 us
    pallas_call x1, Pallas kernels, on_device(): call(functools.partial(backward_kernel, 8), 'attention_backward', jax.Sha...  10.9 us
    all_gather x1, waiting for transfers between devices, on_device(): w_full = lax.all_gather(w_out[0], ('z', 'core'), axis=0, tiled=True)  8.82 us
    pallas_call x1, Pallas kernels, on_device(): call(functools.partial(forward_kernel, 8), 'attention_forward', jax.Shape...  8.47 us
    pallas_call x1, Pallas kernels, on_device(): call(grad_kernel, 'grad_attended', jax.ShapeDtypeStruct((N_SEQ, TOK, PAIR...  5.81 us
    pallas_call x1, Pallas kernels, on_device(): call(project_kernel, 'project', jax.ShapeDtypeStruct((TOK, D), BF16), [vm...  4.25 us
  transfers between devices with their start and end apart: 8, of which 5 were waited for; matrix products, arithmetic and copies ran while one was open for 2% of the time, Pallas kernels for 19%

profile of v4, /device:TPU:8, one launch (start us, length us, event | category | flops | bytes accessed | tf_op | source)
XLA Modules:
  0.0 169.3 jit_solution(13250019503957974288)
XLA Ops:
  7.9 1.2 copy.18
  9.7 1.4 maximum_bitcast_fusion
  11.1 5.9 %all-to-all-start = ((bf16[8,3,128,256]{3,2,1,0:T(8,128)(2,1)}), bf16[8,3,128,256]{3,2,1,0:T(8,128)(2,1)S(1)}, u32[]{:S(2)}, u32[]{:S(2)}) async-start(bf16[8,3,128,256]{3,2,1,0:T(8,128)(2,1)} %maximum_bitcast_fusion), calls=%async_computation | async-start | bytes 3145728 | tf_op jit(solution)/shard_map/to_heads/all_to_all | solution.py:274
  17.2 21.5 %all-to-all-done = bf16[8,3,128,256]{3,2,1,0:T(8,128)(2,1)S(1)} async-done(((bf16[8,3,128,256]{3,2,1,0:T(8,128)(2,1)}), bf16[8,3,128,256]{3,2,1,0:T(8,128)(2,1)S(1)}, u32[]{:S(2)}, u32[]{:S(2)}) %all-to-all-start) | async-done | bytes 1572896 | tf_op jit(solution)/shard_map/to_heads/all_to_all | solution.py:274
  38.6 8.5 %attention_forward.1 = bf16[8,2,64,256]{3,2,1,0:T(8,128)(2,1)S(1)} custom-call(s32[2]{0:T(128)S(1)} %bitcast.33, s32[48]{0:T(128)S(1)} %reshape_squeeze.3.rand_ref, bf16[8,3,2,64,256]{4,3,2,1,0:T(8,128)(2,1)S(1)} %bitcast.26), custom_call_target="tpu_custom_call" | custom-call | flops 1000000000 | bytes 2000000 | tf_op jit(solution)/shard_map/forward/attention_forward/pallas_call | solution.py:292
  47.1 12.7 %all_to_all.30.att_ref.own_ref = bf16[8,128,256]{2,1,0:T(8,128)(2,1)S(1)} all-to-all(bf16[8,128,256]{2,1,0:T(8,128)(2,1)S(1)} %bitcast.32), channel_id=1, replica_groups=mesh['z'=8,'core'=2,'seq'=8,'section'=2] {'seq'}, dimensions={0} | all-to-all | bytes 1048576 | tf_op jit(solution)/shard_map/to_tokens/all_to_all | solution.py:274
  59.8 8.8 %all-gather.3.cloned.1.call-done = bf16[1,2048,2048]{2,1,0:T(8,128)(2,1)} async-done(((bf16[1,128,2048]{2,1,0:T(8,128)(2,1)}), bf16[1,2048,2048]{2,1,0:T(8,128)(2,1)}) %all-gather.3.cloned.1.call-update) | async-done | bytes 8388624 | tf_op jit(solution)/shard_map/gather_w/all_gather | solution.py:284
  68.7 1.0 copy-done.1
  69.7 4.3 %project.1.own_sum_ref.sum_ref = bf16[128,2048]{1,0:T(8,128)(2,1)S(1)} custom-call(bf16[8,128,256]{2,1,0:T(8,128)(2,1)S(1)} %all_to_all.30.att_ref.own_ref, bf16[2048,2048]{1,0:T(8,128)(2,1)} %bitcast.35, bf16[128,2048]{1,0:T(8,128)(2,1)S(1)} %bitcast.29, bf16[128,2048]{1,0:T(8,128)(2,1)S(1)} %bitcast.30, f32[1,2048]{1,0:T(1,128)S(1)} %copy-done.2), custom_call_target="tpu_custom_call" | custom-call | flops 1000000000 | bytes 9000000 | tf_op jit(solution)/shard_map/project/project/pallas_call | solution.py:307
  74.3 1.7 collective-permute-done.1.other_sum_ref
  76.0 3.4 %weight_term.1 = bf16[8,8,128,256]{3,2,1,0:T(8,128)(2,1)} custom-call(s32[1]{0:T(128)} %bitcast.core_ref, bf16[8,128,256]{2,1,0:T(8,128)(2,1)S(1)} %all_to_all.30.att_ref.own_ref, bf16[8,128,256]{2,1,0:T(8,128)(2,1)} %collective-permute-done.other_ref, bf16[128,2048]{1,0:T(8,128)(2,1)S(1)} %project.1.own_sum_ref.sum_ref, ...), custom_call_target="tpu_custom_call" | custom-call | flops 1000000000 | bytes 6000000 | tf_op jit(solution)/shard_map/weight_grad/weight_term/pallas_call | solution.py:334
  79.4 5.8 %grad_attended.1 = bf16[8,128,256]{2,1,0:T(8,128)(2,1)} custom-call(bf16[128,2048]{1,0:T(8,128)(2,1)S(1)} %project.1.own_sum_ref.sum_ref, bf16[2048,2048]{1,0:T(8,128)(2,1)} %bitcast.36), custom_call_target="tpu_custom_call" | custom-call | flops 1000000000 | bytes 9000000 | tf_op jit(solution)/shard_map/project/grad_attended/pallas_call | solution.py:317
  85.3 5.7 %all-to-all-start.2 = ((bf16[8,128,256]{2,1,0:T(8,128)(2,1)}), bf16[8,128,256]{2,1,0:T(8,128)(2,1)S(1)}, u32[]{:S(2)}, u32[]{:S(2)}) async-start(bf16[8,128,256]{2,1,0:T(8,128)(2,1)} %grad_attended.1), calls=%async_computation.3 | async-start | bytes 1048576 | tf_op jit(solution)/shard_map/grad_to_heads/all_to_all | solution.py:274
  91.0 2.1 %collective-permute-start.2 = (bf16[128,2048]{1,0:T(8,128)(2,1)S(1)}, bf16[128,2048]{1,0:T(8,128)(2,1)S(1)}, u32[]{:S(2)}, u32[]{:S(2)}) collective-permute-start(bf16[128,2048]{1,0:T(8,128)(2,1)S(1)} %project.1.own_sum_ref.sum_ref), channel_id=1, source_target_pairs={{0,1},{1,0},{2,3},{3,2},{4,5},{5,4},{6,7},{7,6},{8,9},{9,8},{10,11... | collective-permute-start | bytes 1572872 | tf_op jit(solution)/shard_map/passed/ppermute | solution.py:351
  93.1 7.2 %all-to-all-done.2 = bf16[8,128,256]{2,1,0:T(8,128)(2,1)S(1)} async-done(((bf16[8,128,256]{2,1,0:T(8,128)(2,1)}), bf16[8,128,256]{2,1,0:T(8,128)(2,1)S(1)}, u32[]{:S(2)}, u32[]{:S(2)}) %all-to-all-start.2) | async-done | bytes 524320 | tf_op jit(solution)/shard_map/grad_to_heads/all_to_all | solution.py:274
  100.3 10.9 %attention_backward.1 = bf16[8,3,2,64,256]{4,3,2,1,0:T(8,128)(2,1)S(1)} custom-call(s32[2]{0:T(128)S(1)} %bitcast.34, s32[48]{0:T(128)S(1)} %reshape_squeeze.3.rand_ref, bf16[8,3,2,64,256]{4,3,2,1,0:T(8,128)(2,1)S(1)} %bitcast.27, bf16[8,2,64,256]{3,2,1,0:T(8,128)(2,1)S(1)} %bitcast.31), custom_call_target="tpu_custom_call" | custom-call | flops 3000000000 | bytes 4000000 | tf_op jit(solution)/shard_map/backward/attention_backward/pallas_call | solution.py:354
  111.2 25.5 %all_to_all.31.back_hbm = bf16[8,3,128,256]{3,2,1,0:T(8,128)(2,1)S(1)} all-to-all(bf16[8,3,128,256]{3,2,1,0:T(8,128)(2,1)S(1)} %bitcast.28), channel_id=1, replica_groups=mesh['z'=8,'core'=2,'seq'=8,'section'=2] {'seq'}, dimensions={0} | all-to-all | bytes 3145728 | tf_op jit(solution)/shard_map/grads_to_tokens/all_to_all | solution.py:274
  136.7 12.1 %all_to_all.32.parts_ref = bf16[8,128,256]{2,1,0:T(8,128)(2,1)S(1)} all-to-all(bf16[8,128,256]{2,1,0:T(8,128)(2,1)} %bitcast.42), channel_id=1, replica_groups=mesh['z'=8,'core'=2,'seq'=8,'section'=2] {'seq'}, dimensions={0} | all-to-all | bytes 1048576 | tf_op jit(solution)/shard_map/weight_grad/all_to_all | solution.py:274
  148.7 0.9 weight_sum.1
  149.6 4.2 %all-to-all-start.5 = ((bf16[8,128,256]{2,1,0:T(8,128)(2,1)}), bf16[8,128,256]{2,1,0:T(8,128)(2,1)S(1)}, u32[]{:S(2)}, u32[]{:S(2)}) async-start(bf16[8,128,256]{2,1,0:T(8,128)(2,1)} %weight_sum.1), calls=%async_computation.6 | async-start | bytes 1048576 | tf_op jit(solution)/shard_map/weight_grad/all_to_all | solution.py:274
  153.8 0.8 copied.1
  154.6 1.3 unpack.1
  155.9 5.5 %all-to-all-done.5.pieces_ref = bf16[8,128,256]{2,1,0:T(8,128)(2,1)S(1)} async-done(((bf16[8,128,256]{2,1,0:T(8,128)(2,1)}), bf16[8,128,256]{2,1,0:T(8,128)(2,1)S(1)}, u32[]{:S(2)}, u32[]{:S(2)}) %all-to-all-start.5) | async-done | bytes 524320 | tf_op jit(solution)/shard_map/weight_grad/all_to_all | solution.py:274
  161.4 1.0 average.1
  (25 shorter events, 1.9 us)
Async XLA Ops:
  7.2 2.0 %copy-start.4 = (bf16[1,1,2,128,2048]{4,3,2,1,0:T(8,128)(2,1)S(1)}, bf16[1,1,2,128,2048]{4,3,2,1,0:T(8,128)(2,1)}, u32[]{:S(2)}) copy-start(bf16[1,1,2,128,2048]{4,3,2,1,0:T(8,128)(2,1)} %param.9) | copy-start | bytes 3145732
  7.2 61.5 %all-gather.3.cloned.1.call-start = ((), (), s32[]{:S(2)}) async-start(), calls=%async_computation.8 | async-start | bytes 8912896 | tf_op jit(solution)/shard_map/gather_w/all_gather | solution.py:284
  11.1 5.9 %copy-start.5 = (s32[1,16,3]{1,0,2:T(1,128)S(1)}, s32[1,16,3]{1,0,2:T(1,128)}, u32[]{:S(2)}) copy-start(s32[1,16,3]{1,0,2:T(1,128)} %param.15) | copy-start | bytes 580
  11.1 27.6 %copy-start.3 = (s32[1,2]{1,0:T(1,128)S(1)}, s32[1,2]{1,0:T(1,128)}, u32[]{:S(2)}) copy-start(s32[1,2]{1,0:T(1,128)} %param.14) | copy-start | bytes 28
  11.1 27.5 %all-to-all-start = ((bf16[8,3,128,256]{3,2,1,0:T(8,128)(2,1)}), bf16[8,3,128,256]{3,2,1,0:T(8,128)(2,1)S(1)}, u32[]{:S(2)}, u32[]{:S(2)}) async-start(bf16[8,3,128,256]{3,2,1,0:T(8,128)(2,1)} %maximum_bitcast_fusion), calls=%async_computation | async-start | bytes 3145728 | tf_op jit(solution)/shard_map/to_heads/all_to_all | solution.py:274
  17.0 119.7 %reduce-scatter.2.cloned.1.call-start = ((), (), s32[]{:S(2)}) async-start(), calls=%async_computation.7 | async-start | bytes 4718592 | tf_op jit(solution)/shard_map/weight_grad/reduce_scatter | solution.py:348
  38.6 30.0 %copy-start = (bf16[1,1,128,2048]{3,2,1,0:T(8,128)(2,1)S(1)}, bf16[1,1,128,2048]{3,2,1,0:T(8,128)(2,1)}, u32[]{:S(2)}) copy-start(bf16[1,1,128,2048]{3,2,1,0:T(8,128)(2,1)} %param.10) | copy-start | bytes 1572868
  38.6 30.0 %copy-start.2 = (f32[1,2048]{1,0:T(1,128)S(1)}, f32[1,2048]{1,0:T(1,128)}, u32[]{:S(2)}) copy-start(f32[1,2048]{1,0:T(1,128)} %gain_ref.1) | copy-start | bytes 24580
  59.8 14.5 %collective-permute-start = (bf16[8,128,256]{2,1,0:T(8,128)(2,1)S(1)}, bf16[8,128,256]{2,1,0:T(8,128)(2,1)}, u32[]{:S(2)}, u32[]{:S(2)}) collective-permute-start(bf16[8,128,256]{2,1,0:T(8,128)(2,1)S(1)} %all_to_all.30.att_ref.own_ref), channel_id=1, source_target_pairs={{0,16},{16,0},{1,17},{17,1},{2,18},{18,2},{3,19},{19,3},{4,20},{20... | collective-permute-start | bytes 1572872 | tf_op jit(solution)/shard_map/weight_grad/ppermute | solution.py:332
  68.7 1.0 copy-start.1
  74.0 2.0 %collective-permute-start.1 = (bf16[128,2048]{1,0:T(8,128)(2,1)S(1)}, bf16[128,2048]{1,0:T(8,128)(2,1)S(1)}, u32[]{:S(2)}, u32[]{:S(2)}) collective-permute-start(bf16[128,2048]{1,0:T(8,128)(2,1)S(1)} %project.1.own_sum_ref.sum_ref), channel_id=1, source_target_pairs={{0,16},{16,0},{1,17},{17,1},{2,18},{18,2},{3,19},{19,3},{4,20},{20... | collective-permute-start | bytes 1572872 | tf_op jit(solution)/shard_map/weight_grad/ppermute | solution.py:333
  85.3 15.0 %all-to-all-start.2 = ((bf16[8,128,256]{2,1,0:T(8,128)(2,1)}), bf16[8,128,256]{2,1,0:T(8,128)(2,1)S(1)}, u32[]{:S(2)}, u32[]{:S(2)}) async-start(bf16[8,128,256]{2,1,0:T(8,128)(2,1)} %grad_attended.1), calls=%async_computation.3 | async-start | bytes 1048576 | tf_op jit(solution)/shard_map/grad_to_heads/all_to_all | solution.py:274
  91.0 20.2 %collective-permute-start.2 = (bf16[128,2048]{1,0:T(8,128)(2,1)S(1)}, bf16[128,2048]{1,0:T(8,128)(2,1)S(1)}, u32[]{:S(2)}, u32[]{:S(2)}) collective-permute-start(bf16[128,2048]{1,0:T(8,128)(2,1)S(1)} %project.1.own_sum_ref.sum_ref), channel_id=1, source_target_pairs={{0,1},{1,0},{2,3},{3,2},{4,5},{5,4},{6,7},{7,6},{8,9},{9,8},{10,11... | collective-permute-start | bytes 1572872 | tf_op jit(solution)/shard_map/passed/ppermute | solution.py:351
  149.6 11.8 %all-to-all-start.5 = ((bf16[8,128,256]{2,1,0:T(8,128)(2,1)}), bf16[8,128,256]{2,1,0:T(8,128)(2,1)S(1)}, u32[]{:S(2)}, u32[]{:S(2)}) async-start(bf16[8,128,256]{2,1,0:T(8,128)(2,1)} %weight_sum.1), calls=%async_computation.6 | async-start | bytes 1048576 | tf_op jit(solution)/shard_map/weight_grad/all_to_all | solution.py:274
Sparse Core Ops, SparseCore 0:
  9.8 58.7 all-gather.2
  79.6 53.8 reduce-scatter.1

commit v5 on v4

--- a/solution.py
+++ b/solution.py
@@ -169,7 +169,7 @@
             ga_ref[s] = part.astype(BF16)
 
 
-def term_kernel(core_ref, own_ref, other_ref, own_sum_ref, other_sum_ref, out_hbm, held, sums, sems):
+def term_kernel(core_ref, own_ref, other_ref, own_sum_ref, other_sum_ref, after, out_hbm, held, sums, sems):
     columns = pl.ds(pl.multiple_of(core_ref[0] * HDIM, HDIM), HDIM)
     sums[:TOK] = own_sum_ref[...]
     sums[TOK:] = other_sum_ref[...]
@@ -335,7 +335,7 @@
             term_kernel,
             "weight_term",
             jax.ShapeDtypeStruct((N_Z, N_SEQ, HDIM, PAIR), BF16),
-            [smem()] + [vmem()] * 4,
+            [smem()] + [vmem()] * 4 + [anywhere()],
             anywhere(),
             [
                 pltpu.VMEM((N_Z, N_SEQ, HDIM, PAIR), BF16),
@@ -344,7 +344,7 @@
             ],
             flops=1_000_000_000,
             moved=6_000_000,
-        )(core.reshape(1).astype(jnp.int32), att, other, grad_sum, other_sum)
+        )(core.reshape(1).astype(jnp.int32), att, other, grad_sum, other_sum, grad_att)
         shard = lax.psum_scatter(term, "z", scatter_dimension=0, tiled=True)[0]
 
     with jax.named_scope("passed"):

time: 170 us -> 174 us (1.024)
  blocking collectives: 50.3 us -> 52.9 us
    all_to_all x3, blocking collectives: 50.3 us -> 52.9 us  [exchange(): return lax.all_to_all(chunks, 'seq', 0, 0, tiled=True)]
    reduce_scatter x1, waiting for transfers between devices: 0.01 us -> 2.61 us  [on_device(): shard = lax.psum_scatter(term, 'z', scatter_dimension=0, tiled=True)[0]]
  transfers between devices with their start and end apart: 8 -> 8, of which waited for: 5 -> 5; matrix products, arithmetic and copies ran while one was open for 2% -> 2% of each run, Pallas kernels for 19% -> 18%
where the time goes in v5:
time: 174 us; the launch traced here: 173 us
  blocking collectives  52.9 us (30%)
  waiting for transfers between devices  45.6 us (26%)
  Pallas kernels  36.7 us (21%)
  starting transfers between devices  18.3 us (11%)
  between operations  14.2 us (8%)
  local copies, waits for them, and re-layouts  3.99 us (2%)
    all_to_all x3, blocking collectives, exchange(): return lax.all_to_all(chunks, 'seq', 0, 0, tiled=True)  52.9 us
    all_to_all x3, waiting for transfers between devices, exchange(): return lax.all_to_all(chunks, 'seq', 0, 0, tiled=True)  34.5 us
    all_to_all x3, starting transfers between devices, exchange(): return lax.all_to_all(chunks, 'seq', 0, 0, tiled=True)  15.8 us
    pallas_call x1, Pallas kernels, on_device(): call(functools.partial(backward_kernel, 8), 'attention_backward', jax.Sha...  10.9 us
    pallas_call x1, Pallas kernels, on_device(): call(functools.partial(forward_kernel, 8), 'attention_forward', jax.Shape...  8.47 us
    all_gather x1, waiting for transfers between devices, on_device(): w_full = lax.all_gather(w_out[0], ('z', 'core'), axis=0, tiled=True)  7.84 us
    pallas_call x1, Pallas kernels, on_device(): call(grad_kernel, 'grad_attended', jax.ShapeDtypeStruct((N_SEQ, TOK, PAIR...  5.81 us
    pallas_call x1, Pallas kernels, on_device(): call(project_kernel, 'project', jax.ShapeDtypeStruct((TOK, D), BF16), [vm...  4.25 us
  transfers between devices with their start and end apart: 8, of which 5 were waited for; matrix products, arithmetic and copies ran while one was open for 2% of the time, Pallas kernels for 18%

profile of v5, /device:TPU:8, one launch (start us, length us, event | category | flops | bytes accessed | tf_op | source)
XLA Modules:
  0.0 173.1 jit_solution(2752700929342349512)
XLA Ops:
  7.9 1.5 copy.19
  9.7 0.8 copy-done.4
  10.7 1.4 maximum_bitcast_fusion
  12.1 5.9 %all-to-all-start = ((bf16[8,3,128,256]{3,2,1,0:T(8,128)(2,1)}), bf16[8,3,128,256]{3,2,1,0:T(8,128)(2,1)S(1)}, u32[]{:S(2)}, u32[]{:S(2)}) async-start(bf16[8,3,128,256]{3,2,1,0:T(8,128)(2,1)} %maximum_bitcast_fusion), calls=%async_computation | async-start | bytes 3145728 | tf_op jit(solution)/shard_map/to_heads/all_to_all | solution.py:274
  18.1 21.5 %all-to-all-done = bf16[8,3,128,256]{3,2,1,0:T(8,128)(2,1)S(1)} async-done(((bf16[8,3,128,256]{3,2,1,0:T(8,128)(2,1)}), bf16[8,3,128,256]{3,2,1,0:T(8,128)(2,1)S(1)}, u32[]{:S(2)}, u32[]{:S(2)}) %all-to-all-start) | async-done | bytes 1572896 | tf_op jit(solution)/shard_map/to_heads/all_to_all | solution.py:274
  39.6 8.5 %attention_forward.1 = bf16[8,2,64,256]{3,2,1,0:T(8,128)(2,1)S(1)} custom-call(s32[2]{0:T(128)S(1)} %bitcast.33, s32[48]{0:T(128)S(1)} %reshape_squeeze.3.rand_ref, bf16[8,3,2,64,256]{4,3,2,1,0:T(8,128)(2,1)S(1)} %bitcast.26), custom_call_target="tpu_custom_call" | custom-call | flops 1000000000 | bytes 2000000 | tf_op jit(solution)/shard_map/forward/attention_forward/pallas_call | solution.py:292
  48.1 12.7 %all_to_all.30.att_ref.own_ref = bf16[8,128,256]{2,1,0:T(8,128)(2,1)S(1)} all-to-all(bf16[8,128,256]{2,1,0:T(8,128)(2,1)S(1)} %bitcast.32), channel_id=1, replica_groups=mesh['z'=8,'core'=2,'seq'=8,'section'=2] {'seq'}, dimensions={0} | all-to-all | bytes 1048576 | tf_op jit(solution)/shard_map/to_tokens/all_to_all | solution.py:274
  60.8 7.8 %all-gather.3.cloned.1.call-done = bf16[1,2048,2048]{2,1,0:T(8,128)(2,1)} async-done(((bf16[1,128,2048]{2,1,0:T(8,128)(2,1)}), bf16[1,2048,2048]{2,1,0:T(8,128)(2,1)}) %all-gather.3.cloned.1.call-update) | async-done | bytes 8388624 | tf_op jit(solution)/shard_map/gather_w/all_gather | solution.py:284
  68.7 1.0 copy-done.1
  69.7 4.2 %project.1.sum_ref.own_sum_ref = bf16[128,2048]{1,0:T(8,128)(2,1)S(1)} custom-call(bf16[8,128,256]{2,1,0:T(8,128)(2,1)S(1)} %all_to_all.30.att_ref.own_ref, bf16[2048,2048]{1,0:T(8,128)(2,1)} %bitcast.35, bf16[128,2048]{1,0:T(8,128)(2,1)S(1)} %bitcast.29, bf16[128,2048]{1,0:T(8,128)(2,1)S(1)} %bitcast.30, f32[1,2048]{1,0:T(1,128)S(1)} %copy-done.2), custom_call_target="tpu_custom_call" | custom-call | flops 1000000000 | bytes 9000000 | tf_op jit(solution)/shard_map/project/project/pallas_call | solution.py:307
  74.3 5.8 %grad_attended.1.after = bf16[8,128,256]{2,1,0:T(8,128)(2,1)} custom-call(bf16[128,2048]{1,0:T(8,128)(2,1)S(1)} %project.1.sum_ref.own_sum_ref, bf16[2048,2048]{1,0:T(8,128)(2,1)} %bitcast.36), custom_call_target="tpu_custom_call" | custom-call | flops 1000000000 | bytes 9000000 | tf_op jit(solution)/shard_map/project/grad_attended/pallas_call | solution.py:317
  80.1 3.4 %weight_term.1 = bf16[8,8,128,256]{3,2,1,0:T(8,128)(2,1)} custom-call(s32[1]{0:T(128)} %bitcast.core_ref, bf16[8,128,256]{2,1,0:T(8,128)(2,1)S(1)} %all_to_all.30.att_ref.own_ref, bf16[8,128,256]{2,1,0:T(8,128)(2,1)} %collective-permute-done.other_ref, bf16[128,2048]{1,0:T(8,128)(2,1)S(1)} %project.1.sum_ref.own_sum_ref, ...), custom_call_target="tpu_custom_call" | custom-call | flops 1000000000 | bytes 6000000 | tf_op jit(solution)/shard_map/weight_grad/weight_term/pallas_call | solution.py:334
  83.6 5.7 %all-to-all-start.2 = ((bf16[8,128,256]{2,1,0:T(8,128)(2,1)}), bf16[8,128,256]{2,1,0:T(8,128)(2,1)S(1)}, u32[]{:S(2)}, u32[]{:S(2)}) async-start(bf16[8,128,256]{2,1,0:T(8,128)(2,1)} %grad_attended.1.after), calls=%async_computation.3 | async-start | bytes 1048576 | tf_op jit(solution)/shard_map/grad_to_heads/all_to_all | solution.py:274
  89.3 2.1 %collective-permute-start.2 = (bf16[128,2048]{1,0:T(8,128)(2,1)S(1)}, bf16[128,2048]{1,0:T(8,128)(2,1)S(1)}, u32[]{:S(2)}, u32[]{:S(2)}) collective-permute-start(bf16[128,2048]{1,0:T(8,128)(2,1)S(1)} %project.1.sum_ref.own_sum_ref), channel_id=1, source_target_pairs={{0,1},{1,0},{2,3},{3,2},{4,5},{5,4},{6,7},{7,6},{8,9},{9,8},{10,11... | collective-permute-start | bytes 1572872 | tf_op jit(solution)/shard_map/passed/ppermute | solution.py:351
  91.4 7.2 %all-to-all-done.2 = bf16[8,128,256]{2,1,0:T(8,128)(2,1)S(1)} async-done(((bf16[8,128,256]{2,1,0:T(8,128)(2,1)}), bf16[8,128,256]{2,1,0:T(8,128)(2,1)S(1)}, u32[]{:S(2)}, u32[]{:S(2)}) %all-to-all-start.2) | async-done | bytes 524320 | tf_op jit(solution)/shard_map/grad_to_heads/all_to_all | solution.py:274
  98.6 10.9 %attention_backward.1 = bf16[8,3,2,64,256]{4,3,2,1,0:T(8,128)(2,1)S(1)} custom-call(s32[2]{0:T(128)S(1)} %bitcast.34, s32[48]{0:T(128)S(1)} %reshape_squeeze.3.rand_ref, bf16[8,3,2,64,256]{4,3,2,1,0:T(8,128)(2,1)S(1)} %bitcast.27, bf16[8,2,64,256]{3,2,1,0:T(8,128)(2,1)S(1)} %bitcast.31), custom_call_target="tpu_custom_call" | custom-call | flops 3000000000 | bytes 4000000 | tf_op jit(solution)/shard_map/backward/attention_backward/pallas_call | solution.py:354
  109.5 25.5 %all_to_all.31.back_hbm = bf16[8,3,128,256]{3,2,1,0:T(8,128)(2,1)S(1)} all-to-all(bf16[8,3,128,256]{3,2,1,0:T(8,128)(2,1)S(1)} %bitcast.28), channel_id=1, replica_groups=mesh['z'=8,'core'=2,'seq'=8,'section'=2] {'seq'}, dimensions={0} | all-to-all | bytes 3145728 | tf_op jit(solution)/shard_map/grads_to_tokens/all_to_all | solution.py:274
  135.0 2.6 %reduce-scatter.2.cloned.1.call-done = bf16[1,8,128,256]{3,2,1,0:T(8,128)(2,1)} async-done(((bf16[8,8,128,256]{3,2,1,0:T(8,128)(2,1)}), bf16[1,8,128,256]{3,2,1,0:T(8,128)(2,1)}) %reduce-scatter.2.cloned.1.call-update) | async-done | bytes 524304 | tf_op jit(solution)/shard_map/weight_grad/reduce_scatter | solution.py:348
  137.6 14.7 %all_to_all.32.parts_ref = bf16[8,128,256]{2,1,0:T(8,128)(2,1)S(1)} all-to-all(bf16[8,128,256]{2,1,0:T(8,128)(2,1)} %bitcast.42), channel_id=1, replica_groups=mesh['z'=8,'core'=2,'seq'=8,'section'=2] {'seq'}, dimensions={0} | all-to-all | bytes 1048576 | tf_op jit(solution)/shard_map/weight_grad/all_to_all | solution.py:274
  152.3 0.9 weight_sum.1
  153.2 4.2 %all-to-all-start.5 = ((bf16[8,128,256]{2,1,0:T(8,128)(2,1)}), bf16[8,128,256]{2,1,0:T(8,128)(2,1)S(1)}, u32[]{:S(2)}, u32[]{:S(2)}) async-start(bf16[8,128,256]{2,1,0:T(8,128)(2,1)} %weight_sum.1), calls=%async_computation.6 | async-start | bytes 1048576 | tf_op jit(solution)/shard_map/weight_grad/all_to_all | solution.py:274
  158.2 1.3 unpack.1
  159.4 5.8 %all-to-all-done.5.pieces_ref = bf16[8,128,256]{2,1,0:T(8,128)(2,1)S(1)} async-done(((bf16[8,128,256]{2,1,0:T(8,128)(2,1)}), bf16[8,128,256]{2,1,0:T(8,128)(2,1)S(1)}, u32[]{:S(2)}, u32[]{:S(2)}) %all-to-all-start.5) | async-done | bytes 524320 | tf_op jit(solution)/shard_map/weight_grad/all_to_all | solution.py:274
  165.2 1.0 average.1
  (25 shorter events, 2.5 us)
Async XLA Ops:
  7.2 61.5 %all-gather.3.cloned.1.call-start = ((), (), s32[]{:S(2)}) async-start(), calls=%async_computation.8 | async-start | bytes 8912896 | tf_op jit(solution)/shard_map/gather_w/all_gather | solution.py:284
  9.4 1.0 copy-start.4
  12.1 5.9 %copy-start.5 = (s32[1,16,3]{1,0,2:T(1,128)S(1)}, s32[1,16,3]{1,0,2:T(1,128)}, u32[]{:S(2)}) copy-start(s32[1,16,3]{1,0,2:T(1,128)} %param.15) | copy-start | bytes 580
  12.1 27.6 %copy-start.3 = (s32[1,2]{1,0:T(1,128)S(1)}, s32[1,2]{1,0:T(1,128)}, u32[]{:S(2)}) copy-start(s32[1,2]{1,0:T(1,128)} %param.14) | copy-start | bytes 28
  12.1 27.5 %all-to-all-start = ((bf16[8,3,128,256]{3,2,1,0:T(8,128)(2,1)}), bf16[8,3,128,256]{3,2,1,0:T(8,128)(2,1)S(1)}, u32[]{:S(2)}, u32[]{:S(2)}) async-start(bf16[8,3,128,256]{3,2,1,0:T(8,128)(2,1)} %maximum_bitcast_fusion), calls=%async_computation | async-start | bytes 3145728 | tf_op jit(solution)/shard_map/to_heads/all_to_all | solution.py:274
  18.0 119.6 %reduce-scatter.2.cloned.1.call-start = ((), (), s32[]{:S(2)}) async-start(), calls=%async_computation.7 | async-start | bytes 4718592 | tf_op jit(solution)/shard_map/weight_grad/reduce_scatter | solution.py:348
  39.6 29.0 %copy-start = (bf16[1,1,128,2048]{3,2,1,0:T(8,128)(2,1)S(1)}, bf16[1,1,128,2048]{3,2,1,0:T(8,128)(2,1)}, u32[]{:S(2)}) copy-start(bf16[1,1,128,2048]{3,2,1,0:T(8,128)(2,1)} %param.10) | copy-start | bytes 1572868
  39.6 29.0 %copy-start.2 = (f32[1,2048]{1,0:T(1,128)S(1)}, f32[1,2048]{1,0:T(1,128)}, u32[]{:S(2)}) copy-start(f32[1,2048]{1,0:T(1,128)} %gain_ref.1) | copy-start | bytes 24580
  60.8 19.3 %collective-permute-start = (bf16[8,128,256]{2,1,0:T(8,128)(2,1)S(1)}, bf16[8,128,256]{2,1,0:T(8,128)(2,1)}, u32[]{:S(2)}, u32[]{:S(2)}) collective-permute-start(bf16[8,128,256]{2,1,0:T(8,128)(2,1)S(1)} %all_to_all.30.att_ref.own_ref), channel_id=1, source_target_pairs={{0,16},{16,0},{1,17},{17,1},{2,18},{18,2},{3,19},{19,3},{4,20},{20... | collective-permute-start | bytes 1572872 | tf_op jit(solution)/shard_map/weight_grad/ppermute | solution.py:332
  68.7 1.0 copy-start.1
  74.0 6.2 %collective-permute-start.1 = (bf16[128,2048]{1,0:T(8,128)(2,1)S(1)}, bf16[128,2048]{1,0:T(8,128)(2,1)S(1)}, u32[]{:S(2)}, u32[]{:S(2)}) collective-permute-start(bf16[128,2048]{1,0:T(8,128)(2,1)S(1)} %project.1.sum_ref.own_sum_ref), channel_id=1, source_target_pairs={{0,16},{16,0},{1,17},{17,1},{2,18},{18,2},{3,19},{19,3},{4,20},{20... | collective-permute-start | bytes 1572872 | tf_op jit(solution)/shard_map/weight_grad/ppermute | solution.py:333
  83.6 15.1 %all-to-all-start.2 = ((bf16[8,128,256]{2,1,0:T(8,128)(2,1)}), bf16[8,128,256]{2,1,0:T(8,128)(2,1)S(1)}, u32[]{:S(2)}, u32[]{:S(2)}) async-start(bf16[8,128,256]{2,1,0:T(8,128)(2,1)} %grad_attended.1.after), calls=%async_computation.3 | async-start | bytes 1048576 | tf_op jit(solution)/shard_map/grad_to_heads/all_to_all | solution.py:274
  89.3 20.2 %collective-permute-start.2 = (bf16[128,2048]{1,0:T(8,128)(2,1)S(1)}, bf16[128,2048]{1,0:T(8,128)(2,1)S(1)}, u32[]{:S(2)}, u32[]{:S(2)}) collective-permute-start(bf16[128,2048]{1,0:T(8,128)(2,1)S(1)} %project.1.sum_ref.own_sum_ref), channel_id=1, source_target_pairs={{0,1},{1,0},{2,3},{3,2},{4,5},{5,4},{6,7},{7,6},{8,9},{9,8},{10,11... | collective-permute-start | bytes 1572872 | tf_op jit(solution)/shard_map/passed/ppermute | solution.py:351
  153.2 12.0 %all-to-all-start.5 = ((bf16[8,128,256]{2,1,0:T(8,128)(2,1)}), bf16[8,128,256]{2,1,0:T(8,128)(2,1)S(1)}, u32[]{:S(2)}, u32[]{:S(2)}) async-start(bf16[8,128,256]{2,1,0:T(8,128)(2,1)} %weight_sum.1), calls=%async_computation.6 | async-start | bytes 1048576 | tf_op jit(solution)/shard_map/weight_grad/all_to_all | solution.py:274
Sparse Core Ops, SparseCore 0:
  9.8 58.7 all-gather.2
  83.7 53.8 reduce-scatter.1
